TPU v7x, 32 devices: a whole 2x2x4 slice. The times are simulated.
32 devices in a mesh: dp: 8 (over z, y), row: 2 (over core), col: 2 (over x).
Axes of the slice: x: 2, y: 2, z: 4, core: 2. Of those that a mesh axis runs over, the one named last changes fastest.
Arguments:
- hidden_in: bfloat16 [4096, 2, 512], P('dp', 'row', 'col'), may hold values from -6 to 6
- doc_lens: int32 [8, 4], P('dp'), may hold values from 0 to 512, as said below
- norm1_gain: float32 [2, 512], P('row', 'col'), may hold values from 0.1 to 1.9
- wqkv: bfloat16 [2, 512, 3, 2, 512], P(None, 'col', None, 'row'), may hold values from -0.1875 to 0.1875
- wout: bfloat16 [2, 512, 2, 512], P(None, 'col', 'row'), may hold values from -1 to 1
- norm2_gain: float32 [2, 512], P('row', 'col'), may hold values from 0.1 to 1.9
- wi: bfloat16 [2, 512, 2, 2, 1312], P(None, 'col', None, 'row'), may hold values from -0.1875 to 0.1875
- wo: bfloat16 [2, 1312, 2, 512], P(None, 'col', 'row'), may hold values from -0.15625 to 0.15625
- out_grad: bfloat16 [4096, 2, 512], P('dp', 'row', 'col'), may hold values from -6 to 6
Outputs:
- hidden_out: bfloat16 [4096, 2, 512], P('dp', 'row', 'col')
- grad_in: float32 [4096, 2, 512], P('dp', 'row', 'col')
- grad_norm1: float32 [2, 512], P('row', 'col')
- grad_wqkv: float32 [2, 512, 3, 2, 512], P(None, 'col', None, 'row')
- grad_wout: float32 [2, 512, 2, 512], P(None, 'col', 'row')
- grad_norm2: float32 [2, 512], P('row', 'col')
- grad_wi: float32 [2, 512, 2, 2, 1312], P(None, 'col', None, 'row')
- grad_wo: float32 [2, 1312, 2, 512], P(None, 'col', 'row')
Inputs may be any that keep to these rules, and one draw needn't show every extreme that they name: `doc_lens`: row g lists, in order, the lengths of the sequences packed from slot 0 of data group g (a length may be 0); each row sums to at least 256 and at most 512, and in every draw one row is a single sequence of exactly 512 tokens.
All inputs are finite; a program needn't handle non-finite values.
Results may differ from a plain program's by a relative error of at most 0.024.
Values may be sent and summed in bfloat16 or wider, within the bound.
No kernel may reach another device: no remote copies, remote signals or barrier semaphores. Data moves between devices by JAX's collectives and lax.ppermute only.
A program may use at most 128 MiB of HBM per device.

v0:
```python
import functools
import math

import jax
import jax.numpy as jnp
from jax import lax
from jax.experimental import pallas as pl
from jax.experimental.pallas import tpu as pltpu
from jax.sharding import PartitionSpec as P

HD = 64
EPSILON = 1e-05
ROPE_BASE = 160000.0
F32 = jnp.float32
BF = jnp.bfloat16
LATE = (
    "W2", "L2", "L1", "G", "W1", "W2", "L2", "L1", "O", "G", "W2", "L2", "W1", "L1", "O",
    "W2", "L2", "G",
)
NN = ((1,), (0,))
NT = ((1,), (1,))
TN = ((0,), (0,))


def dot(left, right, dims=NN):
    return lax.dot_general(left, right, (dims, ((), ())), preferred_element_type=F32)


def swap(value, axis):
    return lax.ppermute(value, axis, [(0, 1), (1, 0)])


def dp_swap(value, bit):
    size = lax.axis_size("dp")
    return lax.ppermute(value, "dp", [(i, i ^ bit) for i in range(size)])


def ordered(index, mine, other, axis):
    return jnp.where(
        index == 0,
        jnp.concatenate([mine, other], axis),
        jnp.concatenate([other, mine], axis),
    )


def pick(value, index, parts, axis):
    size = value.shape[axis] // parts
    return lax.dynamic_slice_in_dim(value, index * size, size, axis)


def bits_of(size):
    assert size & (size - 1) == 0
    return [1 << k for k in range(size.bit_length() - 1)]


def call(kernel, outs, ids, *args, scratch=()):
    outs = tuple(jax.ShapeDtypeStruct(s, d) for s, d in outs)
    vmem = pl.BlockSpec(memory_space=pltpu.VMEM)
    return pl.pallas_call(
        kernel,
        out_shape=outs,
        in_specs=[pl.BlockSpec(memory_space=pltpu.SMEM)] + [vmem] * len(args),
        out_specs=tuple(vmem for _ in outs),
        scratch_shapes=list(scratch),
        compiler_params=pltpu.CompilerParams(vmem_limit_bytes=36 * 2**20),
        cost_estimate=pl.CostEstimate(
            flops=1024, bytes_accessed=1024, transcendentals=0
        ),
    )(ids, *args)


def lanes(start, size):
    return pl.ds(pl.multiple_of(start, size), size)


def block(a, b, width):
    return lanes((2 * a + b) * width, width)


def normalize(values):
    centred = values - jnp.mean(values, axis=1, keepdims=True)
    scale = lax.rsqrt(jnp.mean(centred * centred, axis=1, keepdims=True) + EPSILON)
    return (centred * scale, scale)


def norm_backward(grad, normal, scale, gain):
    hat = grad * gain
    correction = (
        hat
        - jnp.mean(hat, axis=1, keepdims=True)
        - normal * jnp.mean(hat * normal, axis=1, keepdims=True)
    )
    return scale * correction


def row_steps(count):
    step = 128 if count % 128 == 0 else count
    return [pl.ds(i, step) for i in range(0, count, step)]


def norm_kernel(ids, own, own_x, others, gain, hidden, normed):
    r, c = ids[0], ids[1]
    width = own.shape[1]
    hidden[:, block(r, c, width)] = own[...]
    hidden[:, block(r, 1 - c, width)] = own_x[...]
    hidden[:, block(1 - r, c, width)] = others[0]
    hidden[:, block(1 - r, 1 - c, width)] = others[1]
    for rows in row_steps(own.shape[0]):
        normal, _ = normalize(hidden[rows, :].astype(F32))
        normed[rows, :] = (normal * gain[...]).astype(BF)


def turn(values, lane):
    size = values.shape[1]
    half = HD // 2
    return jnp.where(
        lane % HD < half, -pltpu.roll(values, size - half, 1), pltpu.roll(values, half, 1)
    )


def segments(ids, shape, axis):
    places = lax.broadcasted_iota(jnp.int32, shape, axis)
    total = jnp.zeros(shape, jnp.int32)
    for j in range(6, ids.shape[0]):
        total = total + (places >= ids[j]).astype(jnp.int32)
    return total


def attend_kernel(ids, normed, w_own, got_y, got_n, cosine, sine, qkv, attended, probs):
    c, y = ids[1], ids[2]
    tokens = normed.shape[0]
    width = got_y.shape[2]
    lane = lax.broadcasted_iota(jnp.int32, (tokens, width), 1)
    for s in range(3):
        total = None
        for a, got in ((y, got_y), (1 - y, got_n)):
            part = dot(normed[:, block(a, c, width)], w_own[a, s, :, lanes(c * width, width)])
            part += dot(normed[:, block(a, 1 - c, width)], got[s])
            total = part if total is None else total + part
        if s < 2:
            total = total * cosine[...] + turn(total, lane) * sine[...]
        qkv[:, s * width : (s + 1) * width] = total.astype(BF)
    pair = 2 * HD
    factor = HD**-0.5
    keys_segment = segments(ids, (1, tokens), 1)
    step = min(256, tokens)
    for start in range(0, tokens, step):
        rows = slice(start, start + step)
        same = (segments(ids, (tokens, 1), 0)[rows]) == keys_segment
        low = lax.broadcasted_iota(jnp.int32, (step, pair), 1) < HD
        for h in range(0, width, pair):
            query = qkv[rows, h : h + pair]
            key = qkv[:, width + h : width + h + pair]
            value = qkv[:, 2 * width + h : 2 * width + h + pair]
            results = []
            for side in range(2):
                mine = low if side == 0 else jnp.logical_not(low)
                scores = dot(jnp.where(mine, query, jnp.zeros_like(query)), key, NT) * factor
                scores = jnp.where(same, scores, -1e30)
                raised = jnp.exp(scores - jnp.max(scores, axis=1, keepdims=True))
                weights = (raised / jnp.sum(raised, axis=1, keepdims=True)).astype(BF)
                probs[h // HD + side, rows, :] = weights
                results.append(dot(weights, value))
            attended[rows, h : h + pair] = jnp.where(low, results[0], results[1]).astype(BF)


def attend_back_kernel(ids, qkv, probs, grad, cosine, sine, out):
    tokens = qkv.shape[0]
    width = qkv.shape[1] // 3
    pair = 2 * HD
    factor = HD**-0.5
    low = lax.broadcasted_iota(jnp.int32, (tokens, pair), 1) < HD
    lane = lax.broadcasted_iota(jnp.int32, (tokens, pair), 1)
    for h in range(0, width, pair):
        query = qkv[:, h : h + pair]
        key = qkv[:, width + h : width + h + pair]
        value = qkv[:, 2 * width + h : 2 * width + h + pair]
        top = grad[:, h : h + pair]
        parts = []
        for side in range(2):
            mine = low if side == 0 else jnp.logical_not(low)
            weights = probs[h // HD + side]
            grad_values = dot(weights, top, TN)
            grad_probs = dot(jnp.where(mine, top, jnp.zeros_like(top)), value, NT)
            wide = weights.astype(F32)
            product = wide * grad_probs
            grad_scores = (product - wide * jnp.sum(product, axis=1, keepdims=True)).astype(BF)
            parts.append(
                (
                    dot(grad_scores, key) * factor,
                    dot(grad_scores, query, TN) * factor,
                    grad_values,
                )
            )
        for s in range(3):
            total = jnp.where(low, parts[0][s], parts[1][s])
            if s < 2:
                total = total * cosine[:, :pair] - turn(total, lane) * sine[:, :pair]
            out[:, s * width + h : s * width + h + pair] = total.astype(BF)


def branch_kernel(ids, own, other, wout, out):
    r = ids[0]
    out[...] = (dot(own[...], wout[r]) + dot(other[...], wout[1 - r])).astype(BF)


def ffn_kernel(
    ids, hidden, br_own, br_got, gain, wi, got_y, got_n, gd_own, gd_got, wo, wo_got,
    middle, normed, activated, mix,
):
    r, c, y = ids[0], ids[1], ids[2]
    half = br_own.shape[1]
    width = half // 2
    hid = mix.shape[2]
    here, there = lanes(r * half, half), lanes((1 - r) * half, half)
    middle[:, here] = hidden[:, here].astype(F32) + br_own[...].astype(F32)
    middle[:, there] = hidden[:, there].astype(F32) + br_got[...].astype(F32)
    for rows in row_steps(hidden.shape[0]):
        normal, _ = normalize(middle[rows, :])
        normed[rows, :] = (normal * gain[...]).astype(BF)
    cols = pl.ds(pl.multiple_of(c * hid, 16), hid)
    step = 256
    for start in range(0, hidden.shape[0], step):
        rows = pl.ds(start, step)
        parts = []
        for g in range(2):
            total = dot(normed[rows, block(0, c, width)], wi[0, g, cols, :], NT)
            total += dot(normed[rows, block(1, c, width)], wi[1, g, cols, :], NT)
            total += dot(normed[rows, block(y, 1 - c, width)], got_y[g], NT)
            total += dot(normed[rows, block(1 - y, 1 - c, width)], got_n[g], NT)
            parts.append(total)
        gate, up = parts
        grad = dot(gd_own[rows, :], wo[r], NT) + dot(gd_got[rows, :], wo_got[...], NT)
        cdf = 0.5 + 0.5 * lax.erf(gate * (0.5**0.5))
        pdf = jnp.exp(-0.5 * gate * gate) * ((2.0 * math.pi) ** -0.5)
        gelu = gate * cdf
        activated[rows, :hid] = (gelu * up).astype(BF)
        mix[0, rows, :] = (grad * up * (cdf + gate * pdf)).astype(BF)
        mix[1, rows, :] = (grad * gelu).astype(BF)


def pieces(count, parts):
    size = -(-count // (16 * parts)) * 16
    return size, [min(j * size, count - size) for j in range(parts)]


def wi_kernel(ids, mix, normed, kept_own, sent_own, kept_far, sent_far):
    c, y, z = ids[1], ids[2], ids[4]
    width = normed.shape[1] // 4
    size, starts = pieces(mix.shape[2], kept_own.shape[1])
    outs = (kept_own, sent_own, kept_far, sent_far)
    places = ((y, c), (1 - y, c), (z, 1 - c), (1 - z, 1 - c))
    right = jnp.concatenate([normed[:, block(a, b, width)] for a, b in places], axis=1)
    for g in range(2):
        total = dot(mix[g], right, TN).astype(BF)
        for k, out in enumerate(outs):
            for j, start in enumerate(starts):
                out[g, j] = total[start : start + size, k * width : (k + 1) * width]


def wo_kernel(hid, ids, own, other, down, kept, sent):
    r, y = ids[0], ids[4]
    width = down.shape[1] // 2
    size, starts = pieces(hid, kept.shape[1])
    right = jnp.concatenate([down[:, lanes(l * width, width)] for l in (y, 1 - y)], axis=1)
    for a, ref in ((r, own), (1 - r, other)):
        total = dot(ref[:, :hid], right, TN).astype(BF)
        for k, out in enumerate((kept, sent)):
            for j, start in enumerate(starts):
                out[a, j] = total[start : start + size, k * width : (k + 1) * width]


def down_kernel(ids, own, other, wo, middle, kept, sent):
    r, c = ids[0], ids[1]
    width = kept.shape[1]
    hid = wo.shape[1]
    for b, ref in ((c, kept), (1 - c, sent)):
        cols = lanes(b * width, width)
        total = dot(own[:, :hid], wo[r, :, cols]) + dot(other[:, :hid], wo[1 - r, :, cols])
        if ref is kept:
            total = total + middle[:, block(r, c, width)]
        ref[...] = total.astype(ref.dtype)


def split_sum(ids, work, kept, sent):
    r = ids[0]
    kept[...] = work[r]
    sent[...] = work[1 - r].astype(BF)


def ffn_back_kernel(ids, mix, wi, got_y, got_n, kept, sent, work):
    c, y = ids[1], ids[2]
    width = kept.shape[1] // 2
    hid = mix.shape[2]
    cols = pl.ds(pl.multiple_of(c * hid, 16), hid)
    for a in range(2):
        work[a, :, lanes(c * width, width)] = dot(mix[0], wi[a, 0, cols, :]) + dot(
            mix[1], wi[a, 1, cols, :]
        )
    for a, got in ((y, got_y), (1 - y, got_n)):
        work[a, :, lanes((1 - c) * width, width)] = dot(mix[0], got[0]) + dot(mix[1], got[1])
    split_sum(ids, work, kept, sent)


def qkv_back_kernel(ids, grad, w_own, got_y, got_n, kept, sent, work):
    c, y = ids[1], ids[2]
    width = kept.shape[1] // 2
    for a, got in ((y, got_y), (1 - y, got_n)):
        for b in range(2):
            total = None
            for s in range(3):
                left = grad[:, s * width : (s + 1) * width]
                right = w_own[a, s, :, lanes(c * width, width)] if b == 0 else got[s]
                part = dot(left, right, NT)
                total = part if total is None else total + part
            where = c if b == 0 else 1 - c
            work[a, :, lanes(where * width, width)] = total
    split_sum(ids, work, kept, sent)


def middle_back_kernel(
    ids, g_own, g_got, middle, gain, gd_own, gd_got, wout, wout_got,
    grad_middle, branch_own, attended, gain_grad, work,
):
    r = ids[0]
    half = g_own.shape[1]
    here, there = lanes(r * half, half), lanes((1 - r) * half, half)
    work[:, here] = g_own[...].astype(F32)
    work[:, there] = g_got[...].astype(F32)
    grad_middle[:, here] = gd_own[...].astype(F32)
    grad_middle[:, there] = gd_got[...].astype(F32)
    total = None
    for rows in row_steps(g_own.shape[0]):
        normal, scale = normalize(middle[rows, :])
        grad = work[rows, :]
        grad_middle[rows, :] += norm_backward(grad, normal, scale, gain[...])
        part = jnp.sum(grad * normal, axis=0, keepdims=True)
        total = part if total is None else total + part
    gain_grad[...] = total
    branch_own[...] = grad_middle[:, here].astype(BF)
    other = grad_middle[:, there].astype(BF)
    attended[...] = (
        dot(branch_own[...], wout[r], NT) + dot(other, wout_got[...], NT)
    ).astype(BF)


def input_back_kernel(
    ids, g_own, g_got, hidden, gain, grad_middle, grad_in, gain_grad, work
):
    r, c = ids[0], ids[1]
    half = g_own.shape[1]
    work[:, lanes(r * half, half)] = g_own[...].astype(F32)
    work[:, lanes((1 - r) * half, half)] = g_got[...].astype(F32)
    total = None
    for rows in row_steps(g_own.shape[0]):
        normal, scale = normalize(hidden[rows, :].astype(F32))
        grad = work[rows, :]
        work[rows, :] = grad_middle[rows, :] + norm_backward(grad, normal, scale, gain[...])
        part = jnp.sum(grad * normal, axis=0, keepdims=True)
        total = part if total is None else total + part
    gain_grad[...] = total
    width = half // 2
    split_lanes(grad_in, 0, 0, g_own.shape[0], width // 128, work[:, block(r, c, width)])


def last_kernel(
    ids, normed, proj, att_own, att_got, branch, kept_own, sent_own, kept_far, sent_far
):
    r, c, y = ids[0], ids[1], ids[2]
    count, rows = kept_own.shape[0], kept_own.shape[1]
    side = proj.shape[1]
    for a, near, far in ((y, kept_own, kept_far), (1 - y, sent_own, sent_far)):
        for b, out in ((c, near), (1 - c, far)):
            width = att_own.shape[1]
            total = dot(normed[:, block(a, b, width)], proj[...], TN).astype(BF)
            for j in range(count):
                out[j, :, :side] = total[j * rows : (j + 1) * rows]
        left = jnp.where(r == a, att_own[...], att_got[...])
        total = dot(left, branch[...], TN).astype(BF)
        for j in range(count):
            near[j, :, side:] = total[j * rows : (j + 1) * rows]


def merged(place, first, second):
    count = first.shape[0]
    for m in range(count):
        yield place ^ m, first, m
        yield place ^ (m + count), second, m


def split_lanes(out, rows, start, count, per, value):
    for t in range(value.shape[1] // 128):
        out[pl.ds(rows * per + start + t, count, stride=per), :] = value[
            :, t * 128 : (t + 1) * 128
        ].astype(F32)


def wi_out_kernel(ids, own_first, own_second, far_first, far_second, out):
    c = ids[1]
    size = own_first.shape[1]
    hid = out.shape[2] // 2
    parts = own_first.shape[0] // 2
    for where, base, refs in (
        (c, ids[3], (own_first, own_second)),
        (1 - c, ids[5], (far_first, far_second)),
    ):
        for place, ref, m in merged(base, *refs):
            a, g, j = place // (2 * parts), (place // parts) % 2, place % parts
            start = where * hid + jnp.minimum(j * size, hid - size)
            out[a, g, pl.ds(pl.multiple_of(start, 16), size), :] = ref[m].astype(F32)


def wo_out_kernel(hid, ids, first, second, out):
    size, width = first.shape[1], first.shape[2]
    parts = first.shape[0] // 2
    per = 2 * width // 128
    for place, ref, m in merged(ids[5], first, second):
        l, a, j = place // (2 * parts), (place // parts) % 2, place % parts
        row = a * hid + jnp.minimum(j * size, hid - size)
        split_lanes(out, row, l * (per // 2), size, per, ref[m])


def last_out_kernel(ids, own_first, own_second, far_first, far_second, qkv, wout):
    c = ids[1]
    size = own_first.shape[1]
    side = far_first.shape[2]
    width = side // 3
    per = 2 * width // 128
    for where, refs in ((c, (own_first, own_second)), (1 - c, (far_first, far_second))):
        for place, ref, m in merged(ids[3], *refs):
            row = place * size
            for s in range(3):
                value = ref[m, :, s * width : (s + 1) * width]
                split_lanes(
                    qkv, row, s * per + where * (per // 2), size, 3 * per, value
                )
            if ref.shape[2] > side:
                split_lanes(wout, row, 0, size, per, ref[m, :, side:])


def stream(kept, sent, order, cross):
    index = lax.axis_index("dp")
    for bit, after in zip(order, order[1:]):
        got = yield sent, bit
        mine = lax.bitwise_and(index, after) != 0
        half = kept.shape[0] // 2
        ks, gs = (kept[:half], kept[half:]), (got[:half], got[half:])
        low, high = [(k.astype(F32) + g.astype(F32)).astype(BF) for k, g in zip(ks, gs)]
        sent = jnp.where(mine, low, high)
        kept = jnp.where(mine, high, low)
    got = yield sent, order[-1]
    value = (kept.astype(F32) + got.astype(F32)).astype(BF)
    if cross:
        value = yield value, "col"
    for bit in order[:0:-1]:
        got = yield value, bit
        value = jnp.concatenate([value, got], axis=0)
    got = yield value, order[0]
    return value, got


def small_stream(value, order):
    for bit in order:
        got = yield value, bit
        value = value + got
    return value


def group_sum(kept, sent):
    half = (kept + swap(sent, "row").astype(F32)).astype(BF)
    got = yield half, "col"
    half = (half.astype(F32) + got.astype(F32)).astype(BF)
    return half, swap(half, "row")


def group_steps(kept, sent):
    got = yield sent, "row"
    half = (kept + got.astype(F32)).astype(BF)
    got = yield half, "col"
    half = (half.astype(F32) + got.astype(F32)).astype(BF)
    got = yield half, "row"
    return half, got


class Streams:
    def __init__(self):
        self.work, self.flight, self.done, self.token = {}, {}, {}, None

    def step(self, name, got):
        try:
            value, way = self.work[name].send(got)
        except StopIteration as end:
            self.done[name] = end.value
            self.token = jax.tree.leaves(end.value)[0]
            return
        self.token = value
        self.flight[name] = swap(value, way) if isinstance(way, str) else dp_swap(value, way)

    def add(self, name, steps):
        self.work[name] = steps
        self.step(name, None)

    def run(self, names):
        for name in names:
            self.step(name, self.after(self.flight.pop(name)))

    def after(self, value):
        return lax.optimization_barrier((value, self.token))[0]


def place_of(order):
    index = lax.axis_index("dp").astype(jnp.int32)
    place = jnp.int32(0)
    for bit in order:
        place = 2 * place + (lax.bitwise_and(index, bit) != 0).astype(jnp.int32)
    return place


def shards(hidden_in, doc_lens, norm1_gain, wqkv, wout, norm2_gain, wi, wo, out_grad):
    tokens, _, width = hidden_in.shape
    half, full = 2 * width, 4 * width
    hid = wo.shape[1]
    count = lax.axis_size("dp")
    row, col = lax.axis_index("row"), lax.axis_index("col")
    side = lax.bitwise_and(lax.axis_index("dp"), 1)
    order = bits_of(count)
    ends = jnp.cumsum(doc_lens[0])
    other = order[1:2] + order[:1] + order[2:]
    bit = (lax.bitwise_and(lax.axis_index("dp"), other[0]) != 0).astype(jnp.int32)
    head = [row, col, side, place_of(order), bit, place_of(other)]
    ids = jnp.concatenate([jnp.stack([h.astype(jnp.int32) for h in head]), ends])

    places = jnp.arange(tokens, dtype=jnp.int32)
    passed = ends[None, :] <= places[:, None]
    doc_start = jnp.sum(jnp.where(passed, doc_lens[0][None, :], 0), axis=1)
    occupied = (places < ends[-1]).astype(BF)[:, None]
    frequency = jnp.exp(
        jnp.arange(HD // 2, dtype=F32) * (-2.0 * math.log(ROPE_BASE) / HD)
    )
    angles = (places - doc_start).astype(F32)[:, None] * frequency[None, :]
    tables = lax.optimization_barrier((jnp.cos(angles), jnp.sin(angles)))
    cosine, sine = [jnp.tile(t, (1, 2 * width // HD)) for t in tables]

    own = hidden_in[:, 0, :]
    own_x = swap(own, "col")
    others = swap(jnp.stack([own, own_x]), "row")
    gains = jnp.concatenate([norm1_gain, norm2_gain], axis=0)
    gains = ordered(col, gains, swap(gains, "col"), 1)
    gains = ordered(row, gains, swap(gains, "row"), 1)
    gain_one, gain_two = gains[0:1], gains[1:2]

    w_qkv = wqkv.transpose(0, 2, 3, 1, 4).reshape(2, 3, width, half)
    qkv_send = lax.dynamic_slice(
        w_qkv, (side, 0, 0, (1 - col) * width), (1, 3, width, width)
    )[0]
    qkv_y = swap(qkv_send, "col")
    qkv_n = dp_swap(qkv_y, 1)
    w_in = wi.transpose(0, 2, 3, 4, 1).reshape(2, 2, 2 * hid, width)
    in_send = lax.dynamic_slice(
        w_in, (side, 0, (1 - col) * hid, 0), (1, 2, hid, width)
    )[0]
    grad_own = out_grad[:, 0, :] * occupied
    in_send, grad_own, qkv_y = lax.optimization_barrier((in_send, grad_own, qkv_y))
    in_y = swap(in_send, "col")
    w_down = wo.reshape(2, hid, half)
    down_got = swap(lax.dynamic_index_in_dim(w_down, 1 - row, 0, False), "row")
    w_out = wout.reshape(2, width, half)
    out_got = swap(lax.dynamic_index_in_dim(w_out, 1 - row, 0, False), "row")

    qkv_n, down_got, out_got = lax.optimization_barrier((qkv_n, down_got, out_got))

    grad_x = swap(grad_own, "col")

    hidden, normed_one = call(
        norm_kernel,
        (((tokens, full), BF), ((tokens, full), BF)),
        ids, own, own_x, others, gain_one,
    )
    qkv, attended, probs = call(
        attend_kernel,
        (((tokens, 3 * width), BF), ((tokens, width), BF), ((width // HD, tokens, tokens), BF)),
        ids, normed_one, w_qkv, qkv_y, qkv_n, cosine, sine,
    )
    attended, in_y, grad_x = lax.optimization_barrier((attended, in_y, grad_x))
    in_n = dp_swap(in_y, 1)
    grad_half = ordered(col, grad_own, grad_x, 1)
    grad_other = swap(grad_half, "row")
    attended_got = swap(attended, "row")
    (branch,) = call(
        branch_kernel, (((tokens, half), BF),), ids, attended, attended_got, w_out,
    )
    branch = (branch.astype(F32) + swap(branch, "col").astype(F32)).astype(BF)
    branch_got = swap(branch, "row")

    wide = -(-hid // 128) * 128
    middle, normed_two, activated, mix = call(
        ffn_kernel,
        (
            ((tokens, full), F32), ((tokens, full), BF), ((tokens, wide), BF),
            ((2, tokens, hid), BF),
        ),
        ids, hidden, branch, branch_got, gain_two, w_in, in_y, in_n, grad_half, grad_other,
        w_down, down_got,
    )
    parts = max(count // 4, 1)
    size, _ = pieces(hid, parts)
    streams = Streams()
    blocks = (count // 2, size, width)
    halves = [
        part.reshape(blocks)
        for part in call(
            wi_kernel, (((2, parts, size, width), BF),) * 4, ids, mix, normed_two
        )
    ]
    streams.add("W1", stream(halves[0], halves[1], order, False))
    kept, sent = call(
        ffn_back_kernel,
        (((tokens, half), F32), ((tokens, half), BF)),
        ids, streams.after(mix), w_in, in_y, in_n,
        scratch=[pltpu.VMEM((2, tokens, half), F32)],
    )
    streams.add("C", group_sum(kept, sent))
    activated_got = swap(activated, "row")
    kept, sent = call(
        functools.partial(wo_kernel, hid), (((2, parts, size, width), BF),) * 2,
        ids, activated, streams.after(activated_got), grad_half,
    )
    streams.add("O", stream(kept.reshape(blocks), sent.reshape(blocks), other, False))
    streams.add("W2", stream(halves[2], halves[3], other, True))
    streams.run(["W1", "O", "C"])
    two_own, two_got = streams.done["C"]
    grad_middle, branch_grad, grad_attended, gain_two_grad = call(
        middle_back_kernel,
        (
            ((tokens, full), F32), ((tokens, half), BF), ((tokens, width), BF), ((1, full), F32),
        ),
        ids, two_own, two_got, middle, gain_two, grad_half, grad_other, w_out, out_got,
        scratch=[pltpu.VMEM((tokens, full), F32)],
    )
    (grad_proj,) = call(
        attend_back_kernel,
        (((tokens, 3 * width), BF),),
        ids, qkv, probs, grad_attended, cosine, sine,
    )
    rows = half // count
    near, far = (count // 2, rows, 3 * width + half), (count // 2, rows, 3 * width)
    halves = call(
        last_kernel, ((near, BF), (near, BF), (far, BF), (far, BF)),
        ids, normed_one, grad_proj, attended, attended_got, branch_grad,
    )
    streams.add("L2", stream(halves[2], halves[3], order, True))
    streams.add("L1", stream(halves[0], halves[1], order, False))
    kept, sent = call(
        qkv_back_kernel,
        (((tokens, half), F32), ((tokens, half), BF)),
        ids, streams.after(grad_proj), w_qkv, qkv_y, qkv_n,
        scratch=[pltpu.VMEM((2, tokens, half), F32)],
    )
    streams.add("D", group_steps(kept, sent))
    for _ in range(3):
        streams.run(["O", "W1", "W2", "L2", "L1", "D"])
    one_own, one_got = streams.done["D"]
    grad_in, gain_one_grad = call(
        input_back_kernel,
        (((tokens * width // 128, 128), F32), ((1, full), F32)),
        ids, one_own, one_got, hidden, gain_one, grad_middle,
        scratch=[pltpu.VMEM((tokens, full), F32)],
    )
    mine = 2 * row + col
    small = jnp.concatenate([pick(gain_one_grad, mine, 4, 1), pick(gain_two_grad, mine, 4, 1)])
    kept, sent = call(
        down_kernel,
        (((tokens, width), F32), ((tokens, width), BF)),
        ids, activated, streams.after(activated_got), w_down, middle,
    )
    hidden_out = (kept + swap(sent, "col").astype(F32)).astype(BF)
    streams.add("G", small_stream(small, order))
    if len(order) == 3:
        streams.run(LATE)
    else:
        while streams.flight:
            streams.run(list(streams.flight))
    own_first, own_second = streams.done["W1"]
    far_first, far_second = streams.done["W2"]
    (grad_wi,) = call(
        wi_out_kernel, (((2, 2, 2 * hid, width), F32),),
        ids, own_first, own_second, far_first, far_second,
    )
    grad_wi = grad_wi.reshape(2, 2, 1, 2 * hid, width).transpose(0, 4, 1, 2, 3)
    (grad_wo,) = call(
        functools.partial(wo_out_kernel, hid), (((2 * hid * half // 128, 128), F32),),
        ids, *streams.done["O"],
    )
    grad_wqkv, grad_wout = call(
        last_out_kernel,
        (((half * 3 * half // 128, 128), F32), ((half * half // 128, 128), F32)),
        ids, *streams.done["L1"], *streams.done["L2"],
    )
    small = streams.done["G"]
    return (
        hidden_out[:, None, :],
        grad_in.reshape(tokens, 1, width),
        small[0:1],
        grad_wqkv.reshape(2, width, 3, 1, half),
        grad_wout.reshape(wout.shape),
        small[1:2],
        grad_wi,
        grad_wo.reshape(wo.shape),
    )


def solution(mesh):
    return jax.shard_map(
        shards,
        mesh=mesh,
        in_specs=(
            P("dp", "row", "col"),
            P("dp", None),
            P("row", "col"),
            P(None, "col", None, "row", None),
            P(None, "col", "row", None),
            P("row", "col"),
            P(None, "col", None, "row", None),
            P(None, "col", "row", None),
            P("dp", "row", "col"),
        ),
        out_specs=(
            P("dp", "row", "col"),
            P("dp", "row", "col"),
            P("row", "col"),
            P(None, "col", None, "row", None),
            P(None, "col", "row", None),
            P("row", "col"),
            P(None, "col", None, "row", None),
            P(None, "col", "row", None),
        ),
        check_vma=False,
    )
```

profile of v0, /device:TPU:0, one launch (start us, length us, event | category | flops | bytes accessed | tf_op | source)
XLA Modules:
  0.0 263.9 jit_solution(4575086261765072659)
XLA Ops:
  16.8 4.1 %collective-permute-done.4.got_y = bf16[3,256,256]{2,1,0:T(8,128)(2,1)} collective-permute-done((bf16[3,256,256]{2,1,0:T(8,128)(2,1)}, bf16[3,256,256]{2,1,0:T(8,128)(2,1)}, u32[]{:S(2)}, u32[]{:S(2)}) %collective-permute-start.4) | collective-permute-done | bytes 393248 | tf_op jit(solution)/shard_map/ppermute | solution.py:30
  39.1 6.1 %shard_map.153 = (bf16[512,768]{1,0:T(8,128)(2,1)S(1)}, bf16[512,256]{1,0:T(8,128)(2,1)S(1)}, bf16[4,512,512]{2,1,0:T(8,128)(2,1)S(1)}) custom-call(s32[10]{0:T(128)S(1)} %concatenate.62.ids, bf16[512,1024]{1,0:T(8,128)(2,1)S(1)} %get-tuple-element.96.normed, bf16[2,3,256,512]{3,2,1,0:T(8,128)(2,1)S(1)} %bitcast.105, ...), custom_call_target="tpu_custom_call" | custom-call | flops 1024 | bytes 1024 | tf_op jit(solution)/shard_map/pallas_call | solution.py:59
  51.0 12.3 %collective-permute-done.11 = bf16[512,512]{1,0:T(8,128)(2,1)S(1)} collective-permute-done((bf16[512,512]{1,0:T(8,128)(2,1)S(1)}, bf16[512,512]{1,0:T(8,128)(2,1)S(1)}, u32[]{:S(2)}, u32[]{:S(2)}) %collective-permute-start.11) | collective-permute-done | bytes 524320 | tf_op jit(solution)/shard_map/ppermute | solution.py:30
  63.5 4.3 %collective-permute-done.13.got_n = bf16[2,656,256]{2,1,0:T(8,128)(2,1)S(1)} collective-permute-done((bf16[2,656,256]{2,1,0:T(8,128)(2,1)}, bf16[2,656,256]{2,1,0:T(8,128)(2,1)S(1)}, u32[]{:S(2)}, u32[]{:S(2)}) %collective-permute-start.13) | collective-permute-done | bytes 671776 | tf_op jit(solution)/shard_map/ppermute | solution.py:35
  67.8 5.2 %shard_map.155 = (f32[512,1024]{1,0:T(8,128)S(1)}, bf16[512,1024]{1,0:T(8,128)(2,1)S(1)}, bf16[512,768]{1,0:T(8,128)(2,1)S(1)}, bf16[2,512,656]{2,1,0:T(8,128)(2,1)S(1)}) custom-call(s32[10]{0:T(128)S(1)} %concatenate.62.ids, bf16[512,1024]{1,0:T(8,128)(2,1)S(1)} %get-tuple-element.95.hidden, bf16[512,512]{1,0:T(8,128)(2,1)S(1)} %add_convert_fusion.4.br_own, ...), custom_call_target="tpu_custom_call" | custom-call | flops 1024 | bytes 1024 | tf_op jit(solution)/shard_map/pallas_call | solution.py:59
  74.3 3.1 %shard_map.156 = (bf16[2,2,336,256]{3,2,1,0:T(8,128)(2,1)S(1)}, bf16[2,2,336,256]{3,2,1,0:T(8,128)(2,1)S(1)}, bf16[2,2,336,256]{3,2,1,0:T(8,128)(2,1)S(1)}, bf16[2,2,336,256]{3,2,1,0:T(8,128)(2,1)}) custom-call(s32[10]{0:T(128)S(1)} %concatenate.62.ids, bf16[2,512,656]{2,1,0:T(8,128)(2,1)S(1)} %get-tuple-element.114.mix, ...), custom_call_target="tpu_custom_call" | custom-call | flops 1024 | bytes 1024 | tf_op jit(solution)/shard_map/pallas_call | solution.py:59
  78.4 3.0 %shard_map.157 = (f32[512,512]{1,0:T(8,128)S(1)}, bf16[512,512]{1,0:T(8,128)(2,1)S(1)}) custom-call(s32[10]{0:T(128)S(1)} %concatenate.62.ids, bf16[2,512,656]{2,1,0:T(8,128)(2,1)S(1)} %get-tuple-element.114.mix, bf16[2,2,1312,256]{3,2,1,0:T(8,128)(2,1)S(1)} %bitcast.101, bf16[2,656,256]{2,1,0:T(8,128)(2,1)} %collective-permute-done.8.got_y, ...), custom_call_target="tpu_custom_call" | custom-call | flops 1024 | bytes 1024 | tf_op jit(solution)/shard_map/pallas_call | solution.py:59
  89.0 10.4 %collective-permute-done.19 = bf16[4,336,256]{2,1,0:T(8,128)(2,1)S(1)} collective-permute-done((bf16[4,336,256]{2,1,0:T(8,128)(2,1)S(1)}, bf16[4,336,256]{2,1,0:T(8,128)(2,1)S(1)}, u32[]{:S(2)}, u32[]{:S(2)}) %collective-permute-start.19) | collective-permute-done | bytes 688160 | tf_op jit(solution)/shard_map/ppermute | solution.py:35
  100.5 3.0 %collective-permute-done.18 = bf16[4,336,256]{2,1,0:T(8,128)(2,1)S(1)} collective-permute-done((bf16[4,336,256]{2,1,0:T(8,128)(2,1)S(1)}, bf16[4,336,256]{2,1,0:T(8,128)(2,1)S(1)}, u32[]{:S(2)}, u32[]{:S(2)}) %collective-permute-start.18) | collective-permute-done | bytes 688160 | tf_op jit(solution)/shard_map/ppermute | solution.py:35
  110.4 3.6 %shard_map.159 = (f32[512,1024]{1,0:T(8,128)S(1)}, bf16[512,512]{1,0:T(8,128)(2,1)S(1)}, bf16[512,256]{1,0:T(8,128)(2,1)S(1)}, f32[1,1024]{1,0:T(1,128)S(1)}) custom-call(s32[10]{0:T(128)S(1)} %concatenate.62.ids, bf16[512,512]{1,0:T(8,128)(2,1)} %add_convert_fusion.2.g_own, bf16[512,512]{1,0:T(8,128)(2,1)} %collective-permute-done.20.g_got, ...), custom_call_target="tpu_custom_call" | custom-call | flops 1024 | bytes 1024 | tf_op jit(solution)/shard_map/pallas_call | solution.py:59
  114.0 4.2 %shard_map.160.proj.grad = bf16[512,768]{1,0:T(8,128)(2,1)S(1)} custom-call(s32[10]{0:T(128)S(1)} %concatenate.62.ids, bf16[512,768]{1,0:T(8,128)(2,1)S(1)} %copy-done.30, bf16[4,512,512]{2,1,0:T(8,128)(2,1)S(1)} %copy-done.25, bf16[512,256]{1,0:T(8,128)(2,1)S(1)} %get-tuple-element.127.grad, f32[512,256]{1,0:T(8,128)S(1)} %copy-done.8, ...), custom_call_target="tpu_custom_call" | custom-call | flops 1024 | bytes 1024 | tf_op jit(solution)/shard_map/pallas_call | solution.py:59
  127.7 7.7 %collective-permute-done.25 = bf16[2,336,256]{2,1,0:T(8,128)(2,1)} collective-permute-done((bf16[2,336,256]{2,1,0:T(8,128)(2,1)}, bf16[2,336,256]{2,1,0:T(8,128)(2,1)}, u32[]{:S(2)}, u32[]{:S(2)}) %collective-permute-start.25) | collective-permute-done | bytes 344096 | tf_op jit(solution)/shard_map/ppermute | solution.py:35
  139.6 6.1 %collective-permute-done.23 = bf16[4,64,768]{2,1,0:T(8,128)(2,1)S(1)} collective-permute-done((bf16[4,64,768]{2,1,0:T(8,128)(2,1)S(1)}, bf16[4,64,768]{2,1,0:T(8,128)(2,1)S(1)}, u32[]{:S(2)}, u32[]{:S(2)}) %collective-permute-start.23) | collective-permute-done | bytes 393248 | tf_op jit(solution)/shard_map/ppermute | solution.py:35
  158.5 6.7 %collective-permute-done.28 = bf16[2,64,1280]{2,1,0:T(8,128)(2,1)S(1)} collective-permute-done((bf16[2,64,1280]{2,1,0:T(8,128)(2,1)S(1)}, bf16[2,64,1280]{2,1,0:T(8,128)(2,1)S(1)}, u32[]{:S(2)}, u32[]{:S(2)}) %collective-permute-start.28) | collective-permute-done | bytes 327712 | tf_op jit(solution)/shard_map/ppermute | solution.py:35
  168.6 12.3 %collective-permute-done.38 = bf16[1,336,256]{2,1,0:T(8,128)(2,1)S(1)} collective-permute-done((bf16[1,336,256]{2,1,0:T(8,128)(2,1)S(1)}, bf16[1,336,256]{2,1,0:T(8,128)(2,1)S(1)}, u32[]{:S(2)}, u32[]{:S(2)}) %collective-permute-start.38) | collective-permute-done | bytes 172064 | tf_op jit(solution)/shard_map/ppermute | solution.py:35
  181.4 3.3 %collective-permute-done.37 = bf16[1,336,256]{2,1,0:T(8,128)(2,1)S(1)} collective-permute-done((bf16[1,336,256]{2,1,0:T(8,128)(2,1)S(1)}, bf16[1,336,256]{2,1,0:T(8,128)(2,1)S(1)}, u32[]{:S(2)}, u32[]{:S(2)}) %collective-permute-start.37) | collective-permute-done | bytes 172064 | tf_op jit(solution)/shard_map/ppermute | solution.py:35
  192.2 3.1 %shard_map.164 = (f32[1024,128]{1,0:T(8,128)}, f32[1,1024]{1,0:T(1,128)S(1)}) custom-call(s32[10]{0:T(128)S(1)} %concatenate.62.ids, bf16[512,512]{1,0:T(8,128)(2,1)S(1)} %add_convert_fusion.g_own, bf16[512,512]{1,0:T(8,128)(2,1)S(1)} %collective-permute-done.34.g_got, bf16[512,1024]{1,0:T(8,128)(2,1)S(1)} %copy-done.12, ...), custom_call_target="tpu_custom_call" | custom-call | flops 1024 | bytes 1024 | tf_op jit(solution)/shard_map/pallas_call | solution.py:59
  196.8 6.1 %collective-permute-done.41 = bf16[1,64,1280]{2,1,0:T(8,128)(2,1)S(1)} collective-permute-done((bf16[1,64,1280]{2,1,0:T(8,128)(2,1)S(1)}, bf16[1,64,1280]{2,1,0:T(8,128)(2,1)S(1)}, u32[]{:S(2)}, u32[]{:S(2)}) %collective-permute-start.41) | collective-permute-done | bytes 163872 | tf_op jit(solution)/shard_map/ppermute | solution.py:35
  206.6 5.5 %collective-permute-done.48 = bf16[1,336,256]{2,1,0:T(8,128)(2,1)S(1)} collective-permute-done((bf16[1,336,256]{2,1,0:T(8,128)(2,1)S(1)}, bf16[1,336,256]{2,1,0:T(8,128)(2,1)S(1)}, u32[]{:S(2)}, u32[]{:S(2)}) %collective-permute-start.48) | collective-permute-done | bytes 172064 | tf_op jit(solution)/shard_map/ppermute | solution.py:35
  213.2 4.1 %collective-permute-done.46 = bf16[2,64,1280]{2,1,0:T(8,128)(2,1)S(1)} collective-permute-done((bf16[2,64,1280]{2,1,0:T(8,128)(2,1)S(1)}, bf16[2,64,1280]{2,1,0:T(8,128)(2,1)S(1)}, u32[]{:S(2)}, u32[]{:S(2)}) %collective-permute-start.46) | collective-permute-done | bytes 327712 | tf_op jit(solution)/shard_map/ppermute | solution.py:35
  219.6 16.0 %collective-permute-done.52 = bf16[2,336,256]{2,1,0:T(8,128)(2,1)S(1)} collective-permute-done((bf16[2,336,256]{2,1,0:T(8,128)(2,1)S(1)}, bf16[2,336,256]{2,1,0:T(8,128)(2,1)S(1)}, u32[]{:S(2)}, u32[]{:S(2)}) %collective-permute-start.52) | collective-permute-done | bytes 344096 | tf_op jit(solution)/shard_map/ppermute | solution.py:35
  237.8 7.7 %collective-permute-done.50 = f32[2,256]{1,0:T(2,128)S(1)} collective-permute-done((f32[2,256]{1,0:T(2,128)S(1)}, f32[2,256]{1,0:T(2,128)S(1)}, u32[]{:S(2)}, u32[]{:S(2)}) %collective-permute-start.50) | collective-permute-done | bytes 2080 | tf_op jit(solution)/shard_map/ppermute | solution.py:35
  246.9 8.3 %collective-permute-done.54.far_second = bf16[4,64,768]{2,1,0:T(8,128)(2,1)S(1)} collective-permute-done((bf16[4,64,768]{2,1,0:T(8,128)(2,1)S(1)}, bf16[4,64,768]{2,1,0:T(8,128)(2,1)S(1)}, u32[]{:S(2)}, u32[]{:S(2)}) %collective-permute-start.54) | collective-permute-done | bytes 393248 | tf_op jit(solution)/shard_map/ppermute | solution.py:35
  260.6 3.4 %shard_map.166 = f32[2,2,1312,256]{3,2,1,0:T(8,128)} custom-call(s32[10]{0:T(128)S(1)} %concatenate.62.ids, bf16[4,336,256]{2,1,0:T(8,128)(2,1)S(1)} %pad_maximum_fusion.own_first, bf16[4,336,256]{2,1,0:T(8,128)(2,1)S(1)} %collective-permute-done.55.own_second, bf16[4,336,256]{2,1,0:T(8,128)(2,1)S(1)} %constant_dynamic-update-slice_fusion.4.far_first, ...), custom_call_target="tpu_custom_call" | custom-call | flops 1024 | bytes 1024 | tf_op jit(solution)/shard_map/pallas_call | solution.py:59
  (255 shorter events, 113.0 us)
Async XLA Ops:
  1.5 20.8 %collective-permute-start.2 = (f32[2,256]{1,0:T(2,128)S(1)}, f32[2,256]{1,0:T(2,128)}, u32[]{:S(2)}, u32[]{:S(2)}) collective-permute-start(f32[2,256]{1,0:T(2,128)S(1)} %pad_maximum_fusion.7), channel_id=1, source_target_pairs={{0,1},{1,0},{2,3},{3,2},{4,5},{5,4},{6,7},{7,6},{8,9},{9,8},{10,11... | collective-permute-start | bytes 6152 | tf_op jit(solution)/shard_map/ppermute | solution.py:30
  10.3 26.4 %collective-permute-start.6 = (bf16[656,512]{1,0:T(8,128)(2,1)}, bf16[656,512]{1,0:T(8,128)(2,1)}, u32[]{:S(2)}, u32[]{:S(2)}) collective-permute-start(bf16[656,512]{1,0:T(8,128)(2,1)} %dynamic-slice_bitcast_fusion), channel_id=1, source_target_pairs={{0,2},{2,0},{1,3},{3,1},{4,6},{6,4},{5,7},{7,5},{8,10},{10,8},{9,1... | collective-permute-start | bytes 2015240 | tf_op jit(solution)/shard_map/ppermute | solution.py:30
  21.0 25.6 %collective-permute-start.8 = (bf16[2,656,256]{2,1,0:T(8,128)(2,1)}, bf16[2,656,256]{2,1,0:T(8,128)(2,1)}, u32[]{:S(2)}, u32[]{:S(2)}) collective-permute-start(bf16[2,656,256]{2,1,0:T(8,128)(2,1)} %dynamic-slice_bitcast_fusion.1), channel_id=1, source_target_pairs={{0,1},{1,0},{2,3},{3,2},{4,5},{5,4},{6,7},{7,6},{8,9},{9,8},{10,11... | collective-permute-start | bytes 2015240 | tf_op jit(solution)/shard_map/ppermute | solution.py:30
  50.0 17.7 %collective-permute-start.13 = (bf16[2,656,256]{2,1,0:T(8,128)(2,1)}, bf16[2,656,256]{2,1,0:T(8,128)(2,1)S(1)}, u32[]{:S(2)}, u32[]{:S(2)}) collective-permute-start(bf16[2,656,256]{2,1,0:T(8,128)(2,1)} %collective-permute-done.8.got_y), channel_id=1, source_target_pairs={{0,4},{4,0},{8,12},{12,8},{16,20},{20,16},{24,28},{28,24},{1,5},{5... | collective-permute-start | bytes 2015240 | tf_op jit(solution)/shard_map/ppermute | solution.py:35
  105.5 18.4 %collective-permute-start.26 = (bf16[2,336,256]{2,1,0:T(8,128)(2,1)}, bf16[2,336,256]{2,1,0:T(8,128)(2,1)}, u32[]{:S(2)}, u32[]{:S(2)}) collective-permute-start(bf16[2,336,256]{2,1,0:T(8,128)(2,1)} %get-tuple-element.211), channel_id=1, source_target_pairs={{0,4},{4,0},{8,12},{12,8},{16,20},{20,16},{24,28},{28,24},{1,5},{5... | collective-permute-start | bytes 1032200 | tf_op jit(solution)/shard_map/ppermute | solution.py:35
  106.4 31.2 %collective-permute-start.24 = (bf16[4,336,256]{2,1,0:T(8,128)(2,1)}, bf16[4,336,256]{2,1,0:T(8,128)(2,1)}, u32[]{:S(2)}, u32[]{:S(2)}) collective-permute-start(bf16[4,336,256]{2,1,0:T(8,128)(2,1)} %bitcast.38), channel_id=1, source_target_pairs={{0,8},{4,12},{8,0},{12,4},{16,24},{20,28},{24,16},{28,20},{1,9},{5... | collective-permute-start | bytes 2064392 | tf_op jit(solution)/shard_map/ppermute | solution.py:35
  108.0 27.3 %collective-permute-start.25 = (bf16[2,336,256]{2,1,0:T(8,128)(2,1)}, bf16[2,336,256]{2,1,0:T(8,128)(2,1)}, u32[]{:S(2)}, u32[]{:S(2)}) collective-permute-start(bf16[2,336,256]{2,1,0:T(8,128)(2,1)} %get-tuple-element.209), channel_id=1, source_target_pairs={{0,8},{4,12},{8,0},{12,4},{16,24},{20,28},{24,16},{28,20},{1,9},{5... | collective-permute-start | bytes 1032200 | tf_op jit(solution)/shard_map/ppermute | solution.py:35
  120.2 26.8 %collective-permute-start.22 = (bf16[4,64,1280]{2,1,0:T(8,128)(2,1)S(1)}, bf16[4,64,1280]{2,1,0:T(8,128)(2,1)S(1)}, u32[]{:S(2)}, u32[]{:S(2)}) collective-permute-start(bf16[4,64,1280]{2,1,0:T(8,128)(2,1)S(1)} %get-tuple-element.129), channel_id=1, source_target_pairs={{0,4},{4,0},{8,12},{12,8},{16,20},{20,16},{24,28},{28,24},{1,5},{5... | collective-permute-start | bytes 1966088 | tf_op jit(solution)/shard_map/ppermute | solution.py:35
  123.8 24.4 %collective-permute-start.21 = (bf16[512,512]{1,0:T(8,128)(2,1)S(1)}, bf16[512,512]{1,0:T(8,128)(2,1)S(1)}, u32[]{:S(2)}, u32[]{:S(2)}) collective-permute-start(bf16[512,512]{1,0:T(8,128)(2,1)S(1)} %get-tuple-element.132), channel_id=1, source_target_pairs={{0,2},{2,0},{1,3},{3,1},{4,6},{6,4},{5,7},{7,5},{8,10},{10,8},{9,1... | collective-permute-start | bytes 1572872 | tf_op jit(solution)/shard_map/ppermute | solution.py:30
  125.0 24.6 %collective-permute-start.32 = (bf16[1,336,256]{2,1,0:T(8,128)(2,1)S(1)}, bf16[1,336,256]{2,1,0:T(8,128)(2,1)S(1)}, u32[]{:S(2)}, u32[]{:S(2)}) collective-permute-start(bf16[1,336,256]{2,1,0:T(8,128)(2,1)S(1)} %broadcast_select_fusion.12), channel_id=1, source_target_pairs={{0,16},{4,20},{8,24},{12,28},{16,0},{20,4},{24,8},{28,12},{1,17},{... | collective-permute-start | bytes 516104 | tf_op jit(solution)/shard_map/ppermute | solution.py:35
  155.3 25.6 %collective-permute-start.38 = (bf16[1,336,256]{2,1,0:T(8,128)(2,1)S(1)}, bf16[1,336,256]{2,1,0:T(8,128)(2,1)S(1)}, u32[]{:S(2)}, u32[]{:S(2)}) collective-permute-start(bf16[1,336,256]{2,1,0:T(8,128)(2,1)S(1)} %add_convert_fusion.13), channel_id=1, source_target_pairs={{0,16},{4,20},{8,24},{12,28},{16,0},{20,4},{24,8},{28,12},{1,17},{... | collective-permute-start | bytes 516104 | tf_op jit(solution)/shard_map/ppermute | solution.py:35
  156.8 27.8 %collective-permute-start.37 = (bf16[1,336,256]{2,1,0:T(8,128)(2,1)S(1)}, bf16[1,336,256]{2,1,0:T(8,128)(2,1)S(1)}, u32[]{:S(2)}, u32[]{:S(2)}) collective-permute-start(bf16[1,336,256]{2,1,0:T(8,128)(2,1)S(1)} %broadcast_select_fusion.10), channel_id=1, source_target_pairs={{0,16},{4,20},{8,24},{12,28},{16,0},{20,4},{24,8},{28,12},{1,17},{... | collective-permute-start | bytes 516104 | tf_op jit(solution)/shard_map/ppermute | solution.py:35
  165.2 21.5 %collective-permute-start.36 = (bf16[1,64,768]{2,1,0:T(8,128)(2,1)S(1)}, bf16[1,64,768]{2,1,0:T(8,128)(2,1)S(1)}, u32[]{:S(2)}, u32[]{:S(2)}) collective-permute-start(bf16[1,64,768]{2,1,0:T(8,128)(2,1)S(1)} %broadcast_select_fusion.14), channel_id=1, source_target_pairs={{0,16},{4,20},{8,24},{12,28},{16,0},{20,4},{24,8},{28,12},{1,17},{... | collective-permute-start | bytes 294920 | tf_op jit(solution)/shard_map/ppermute | solution.py:35
  165.4 23.2 %collective-permute-start.35 = (bf16[1,64,1280]{2,1,0:T(8,128)(2,1)S(1)}, bf16[1,64,1280]{2,1,0:T(8,128)(2,1)S(1)}, u32[]{:S(2)}, u32[]{:S(2)}) collective-permute-start(bf16[1,64,1280]{2,1,0:T(8,128)(2,1)S(1)} %broadcast_select_fusion.13), channel_id=1, source_target_pairs={{0,16},{4,20},{8,24},{12,28},{16,0},{20,4},{24,8},{28,12},{1,17},{... | collective-permute-start | bytes 491528 | tf_op jit(solution)/shard_map/ppermute | solution.py:35
  168.5 22.1 %collective-permute-start.34 = (bf16[512,512]{1,0:T(8,128)(2,1)S(1)}, bf16[512,512]{1,0:T(8,128)(2,1)S(1)}, u32[]{:S(2)}, u32[]{:S(2)}) collective-permute-start(bf16[512,512]{1,0:T(8,128)(2,1)S(1)} %add_convert_fusion.g_own), channel_id=1, source_target_pairs={{0,2},{2,0},{1,3},{3,1},{4,6},{6,4},{5,7},{7,5},{8,10},{10,8},{9,1... | collective-permute-start | bytes 1572872 | tf_op jit(solution)/shard_map/ppermute | solution.py:30
  180.8 36.5 %collective-permute-start.45 = (bf16[2,336,256]{2,1,0:T(8,128)(2,1)S(1)}, bf16[2,336,256]{2,1,0:T(8,128)(2,1)S(1)}, u32[]{:S(2)}, u32[]{:S(2)}) collective-permute-start(bf16[2,336,256]{2,1,0:T(8,128)(2,1)S(1)} %pad_maximum_fusion.4), channel_id=1, source_target_pairs={{0,4},{4,0},{8,12},{12,8},{16,20},{20,16},{24,28},{28,24},{1,5},{5... | collective-permute-start | bytes 1032200 | tf_op jit(solution)/shard_map/ppermute | solution.py:35
  184.6 21.4 %collective-permute-start.49 = (bf16[2,336,256]{2,1,0:T(8,128)(2,1)S(1)}, bf16[2,336,256]{2,1,0:T(8,128)(2,1)S(1)}, u32[]{:S(2)}, u32[]{:S(2)}) collective-permute-start(bf16[2,336,256]{2,1,0:T(8,128)(2,1)S(1)} %pad_maximum_fusion.5), channel_id=1, source_target_pairs={{0,8},{4,12},{8,0},{12,4},{16,24},{20,28},{24,16},{28,20},{1,9},{5... | collective-permute-start | bytes 1032200 | tf_op jit(solution)/shard_map/ppermute | solution.py:35
  195.3 40.8 %collective-permute-start.33 = (bf16[512,256]{1,0:T(8,128)(2,1)S(1)}, bf16[512,256]{1,0:T(8,128)(2,1)S(1)}, u32[]{:S(2)}, u32[]{:S(2)}) collective-permute-start(bf16[512,256]{1,0:T(8,128)(2,1)S(1)} %get-tuple-element.151), channel_id=1, source_target_pairs={{0,1},{1,0},{2,3},{3,2},{4,5},{5,4},{6,7},{7,6},{8,9},{9,8},{10,11... | collective-permute-start | bytes 786440 | tf_op jit(solution)/shard_map/ppermute | solution.py:30
  213.1 33.7 %collective-permute-start.55 = (bf16[4,336,256]{2,1,0:T(8,128)(2,1)S(1)}, bf16[4,336,256]{2,1,0:T(8,128)(2,1)S(1)}, u32[]{:S(2)}, u32[]{:S(2)}) collective-permute-start(bf16[4,336,256]{2,1,0:T(8,128)(2,1)S(1)} %pad_maximum_fusion.own_first), channel_id=1, source_target_pairs={{0,4},{4,0},{8,12},{12,8},{16,20},{20,16},{24,28},{28,24},{1,5},{5... | collective-permute-start | bytes 2064392 | tf_op jit(solution)/shard_map/ppermute | solution.py:35
  217.2 18.4 %collective-permute-start.52 = (bf16[2,336,256]{2,1,0:T(8,128)(2,1)S(1)}, bf16[2,336,256]{2,1,0:T(8,128)(2,1)S(1)}, u32[]{:S(2)}, u32[]{:S(2)}) collective-permute-start(bf16[2,336,256]{2,1,0:T(8,128)(2,1)S(1)} %get-tuple-element.217), channel_id=1, source_target_pairs={{0,4},{4,0},{8,12},{12,8},{16,20},{20,16},{24,28},{28,24},{1,5},{5... | collective-permute-start | bytes 1032200 | tf_op jit(solution)/shard_map/ppermute | solution.py:35
  217.3 18.8 %collective-permute-start.51 = (bf16[2,64,768]{2,1,0:T(8,128)(2,1)S(1)}, bf16[2,64,768]{2,1,0:T(8,128)(2,1)S(1)}, u32[]{:S(2)}, u32[]{:S(2)}) collective-permute-start(bf16[2,64,768]{2,1,0:T(8,128)(2,1)S(1)} %get-tuple-element.221), channel_id=1, source_target_pairs={{0,8},{4,12},{8,0},{12,4},{16,24},{20,28},{24,16},{28,20},{1,9},{5... | collective-permute-start | bytes 589832 | tf_op jit(solution)/shard_map/ppermute | solution.py:35
  217.5 40.6 %collective-permute-start.57 = (bf16[4,336,256]{2,1,0:T(8,128)(2,1)S(1)}, bf16[4,336,256]{2,1,0:T(8,128)(2,1)S(1)}, u32[]{:S(2)}, u32[]{:S(2)}) collective-permute-start(bf16[4,336,256]{2,1,0:T(8,128)(2,1)S(1)} %pad_maximum_fusion.1.first), channel_id=1, source_target_pairs={{0,8},{4,12},{8,0},{12,4},{16,24},{20,28},{24,16},{28,20},{1,9},{5... | collective-permute-start | bytes 2064392 | tf_op jit(solution)/shard_map/ppermute | solution.py:35
  235.6 25.0 %collective-permute-start.56 = (bf16[4,336,256]{2,1,0:T(8,128)(2,1)S(1)}, bf16[4,336,256]{2,1,0:T(8,128)(2,1)S(1)}, u32[]{:S(2)}, u32[]{:S(2)}) collective-permute-start(bf16[4,336,256]{2,1,0:T(8,128)(2,1)S(1)} %constant_dynamic-update-slice_fusion.4.far_first), channel_id=1, source_target_pairs={{0,8},{4,12},{8,0},{12,4},{16,24},{20,28},{24,16},{28,20},{1,9},{5... | collective-permute-start | bytes 2064392 | tf_op jit(solution)/shard_map/ppermute | solution.py:35
  236.2 19.0 %collective-permute-start.53 = (bf16[4,64,1280]{2,1,0:T(8,128)(2,1)S(1)}, bf16[4,64,1280]{2,1,0:T(8,128)(2,1)S(1)}, u32[]{:S(2)}, u32[]{:S(2)}) collective-permute-start(bf16[4,64,1280]{2,1,0:T(8,128)(2,1)S(1)} %pad_maximum_fusion.2.own_first), channel_id=1, source_target_pairs={{0,4},{4,0},{8,12},{12,8},{16,20},{20,16},{24,28},{28,24},{1,5},{5... | collective-permute-start | bytes 1966088 | tf_op jit(solution)/shard_map/ppermute | solution.py:35
  (76 other events, 743.0 us)
where the time goes:
time: 265 us; the launch traced here: 264 us
  waiting for transfers between devices  124 us (47%)
  starting transfers between devices  50.5 us (19%)
  Pallas kernels  47.3 us (18%)
  local copies, waits for them, and re-layouts  22.1 us (8%)
  other arithmetic  18.6 us (7%)
    ppermute x35, waiting for transfers between devices, dp_swap(): return lax.ppermute(value, 'dp', [(i, i ^ bit) for i in range(size)])  105 us
    pallas_call x16, Pallas kernels, call(): pl.pallas_call(kernel, out_shape=outs, in_specs=[pl.BlockSpec(memory_spac...  47.3 us
    ppermute x35, starting transfers between devices, dp_swap(): return lax.ppermute(value, 'dp', [(i, i ^ bit) for i in range(size)])  36.2 us
    ppermute x23, waiting for transfers between devices, swap(): return lax.ppermute(value, axis, [(0, 1), (1, 0)])  19.4 us
    ppermute x23, starting transfers between devices, swap(): return lax.ppermute(value, axis, [(0, 1), (1, 0)])  14.3 us
    unnamed x88, local copies, waits for them, and re-layouts  8.91 us
    another operation x4, local copies, waits for them, and re-layouts, shards(): cosine, sine = [jnp.tile(t, (1, 2 * width // HD)) for t in tables]  5.92 us
  transfers between devices with their start and end apart: 58, of which 22 were waited for; matrix products, arithmetic and copies ran while one was open for 11% of the time, Pallas kernels for 12%

commit v1 on v0

--- a/solution.py
+++ b/solution.py
@@ -14,8 +14,7 @@
 F32 = jnp.float32
 BF = jnp.bfloat16
 LATE = (
-    "W2", "L2", "L1", "G", "W1", "W2", "L2", "L1", "O", "G", "W2", "L2", "W1", "L1", "O",
-    "W2", "L2", "G",
+    "W2", "L2", "L1", "G", "W1", "W2", "G", "L2", "L1", "G", "O", "W2", "W1", "L2",
 )
 NN = ((1,), (0,))
 NT = ((1,), (1,))
@@ -53,7 +52,7 @@
     return [1 << k for k in range(size.bit_length() - 1)]
 
 
-def call(kernel, outs, ids, *args, scratch=()):
+def call(kernel, outs, ids, *args, scratch=(), flops=1024):
     outs = tuple(jax.ShapeDtypeStruct(s, d) for s, d in outs)
     vmem = pl.BlockSpec(memory_space=pltpu.VMEM)
     return pl.pallas_call(
@@ -64,7 +63,7 @@
         scratch_shapes=list(scratch),
         compiler_params=pltpu.CompilerParams(vmem_limit_bytes=36 * 2**20),
         cost_estimate=pl.CostEstimate(
-            flops=1024, bytes_accessed=1024, transcendentals=0
+            flops=flops, bytes_accessed=1024, transcendentals=0
         ),
     )(ids, *args)
 
@@ -131,6 +130,10 @@
     tokens = normed.shape[0]
     width = got_y.shape[2]
     lane = lax.broadcasted_iota(jnp.int32, (tokens, width), 1)
+
+    def wide(table):
+        return jnp.concatenate([table[...]] * (width // table.shape[1]), axis=1)
+
     for s in range(3):
         total = None
         for a, got in ((y, got_y), (1 - y, got_n)):
@@ -138,7 +141,7 @@
             part += dot(normed[:, block(a, 1 - c, width)], got[s])
             total = part if total is None else total + part
         if s < 2:
-            total = total * cosine[...] + turn(total, lane) * sine[...]
+            total = total * wide(cosine) + turn(total, lane) * wide(sine)
         qkv[:, s * width : (s + 1) * width] = total.astype(BF)
     pair = 2 * HD
     factor = HD**-0.5
@@ -195,7 +198,7 @@
         for s in range(3):
             total = jnp.where(low, parts[0][s], parts[1][s])
             if s < 2:
-                total = total * cosine[:, :pair] - turn(total, lane) * sine[:, :pair]
+                total = total * cosine[...] - turn(total, lane) * sine[...]
             out[:, s * width + h : s * width + h + pair] = total.astype(BF)
 
 
@@ -537,14 +540,14 @@
     frequency = jnp.exp(
         jnp.arange(HD // 2, dtype=F32) * (-2.0 * math.log(ROPE_BASE) / HD)
     )
-    angles = (places - doc_start).astype(F32)[:, None] * frequency[None, :]
-    tables = lax.optimization_barrier((jnp.cos(angles), jnp.sin(angles)))
-    cosine, sine = [jnp.tile(t, (1, 2 * width // HD)) for t in tables]
+    angles = (places - doc_start).astype(F32)[:, None] * jnp.tile(frequency, 4)[None, :]
+    cosine, sine = jnp.cos(angles), jnp.sin(angles)
 
     own = hidden_in[:, 0, :]
     own_x = swap(own, "col")
+    gains = jnp.concatenate([norm1_gain, norm2_gain], axis=0)
+    gains, own_x = lax.optimization_barrier((gains, own_x))
     others = swap(jnp.stack([own, own_x]), "row")
-    gains = jnp.concatenate([norm1_gain, norm2_gain], axis=0)
     gains = ordered(col, gains, swap(gains, "col"), 1)
     gains = ordered(row, gains, swap(gains, "row"), 1)
     gain_one, gain_two = gains[0:1], gains[1:2]
@@ -559,7 +562,7 @@
     in_send = lax.dynamic_slice(
         w_in, (side, 0, (1 - col) * hid, 0), (1, 2, hid, width)
     )[0]
-    grad_own = out_grad[:, 0, :] * occupied
+    grad_own = out_grad[:, 0, :]
     in_send, grad_own, qkv_y = lax.optimization_barrier((in_send, grad_own, qkv_y))
     in_y = swap(in_send, "col")
     w_down = wo.reshape(2, hid, half)
@@ -583,7 +586,7 @@
     )
     attended, in_y, grad_x = lax.optimization_barrier((attended, in_y, grad_x))
     in_n = dp_swap(in_y, 1)
-    grad_half = ordered(col, grad_own, grad_x, 1)
+    grad_half = ordered(col, grad_own, grad_x, 1) * occupied
     grad_other = swap(grad_half, "row")
     attended_got = swap(attended, "row")
     (branch,) = call(
@@ -606,6 +609,13 @@
     size, _ = pieces(hid, parts)
     streams = Streams()
     blocks = (count // 2, size, width)
+    kept, sent = call(
+        ffn_back_kernel,
+        (((tokens, half), F32), ((tokens, half), BF)),
+        ids, mix, w_in, in_y, in_n,
+        scratch=[pltpu.VMEM((2, tokens, half), F32)],
+    )
+    mix, sent = lax.optimization_barrier((mix, sent))
     halves = [
         part.reshape(blocks)
         for part in call(
@@ -613,12 +623,6 @@
         )
     ]
     streams.add("W1", stream(halves[0], halves[1], order, False))
-    kept, sent = call(
-        ffn_back_kernel,
-        (((tokens, half), F32), ((tokens, half), BF)),
-        ids, streams.after(mix), w_in, in_y, in_n,
-        scratch=[pltpu.VMEM((2, tokens, half), F32)],
-    )
     streams.add("C", group_sum(kept, sent))
     activated_got = swap(activated, "row")
     kept, sent = call(
@@ -678,19 +682,25 @@
     if len(order) == 3:
         streams.run(LATE)
     else:
-        while streams.flight:
-            streams.run(list(streams.flight))
-    own_first, own_second = streams.done["W1"]
-    far_first, far_second = streams.done["W2"]
-    (grad_wi,) = call(
-        wi_out_kernel, (((2, 2, 2 * hid, width), F32),),
-        ids, own_first, own_second, far_first, far_second,
-    )
-    grad_wi = grad_wi.reshape(2, 2, 1, 2 * hid, width).transpose(0, 4, 1, 2, 3)
+        for name in list(streams.flight):
+            while name in streams.flight:
+                streams.run([name])
+    streams.run([name for name in ("O",) if name in streams.flight])
     (grad_wo,) = call(
         functools.partial(wo_out_kernel, hid), (((2 * hid * half // 128, 128), F32),),
         ids, *streams.done["O"],
-    )
+        flops=8 * 10**9,
+    )
+    streams.token = grad_wo
+    streams.run([name for name in ("W1", "W2") if name in streams.flight])
+    (grad_wi,) = call(
+        wi_out_kernel, (((2, 2, 2 * hid, width), F32),),
+        ids, *streams.done["W1"], *streams.done["W2"],
+        flops=8 * 10**9,
+    )
+    streams.token = grad_wi
+    grad_wi = grad_wi.reshape(2, 2, 1, 2 * hid, width).transpose(0, 4, 1, 2, 3)
+    streams.run([name for name in ("L1", "L2", "G") if name in streams.flight])
     grad_wqkv, grad_wout = call(
         last_out_kernel,
         (((half * 3 * half // 128, 128), F32), ((half * half // 128, 128), F32)),

time: 265 us -> 260 us (0.981)
  waiting for transfers between devices: 124 us -> 113 us
  starting transfers between devices: 50.5 us -> 60.9 us
  other arithmetic: 18.6 us -> 15.3 us
    ppermute x35, starting transfers between devices: 36.2 us -> 46.3 us  [dp_swap(): return lax.ppermute(value, 'dp', [(i, i ^ bit) for i in range(size)])]
    ppermute x35, waiting for transfers between devices: 105 us -> 95.4 us  [dp_swap(): return lax.ppermute(value, 'dp', [(i, i ^ bit) for i in range(size)])]
    another operation x4 -> x1, local copies, waits for them, and re-layouts: 5.92 us -> 0.01 us  [shards(): jnp.tile(frequency, 4)[None, :]]
    unnamed x88 -> x96, local copies, waits for them, and re-layouts: 8.91 us -> 12.5 us
  transfers between devices with their start and end apart: 58 -> 58, of which waited for: 22 -> 22; matrix products, arithmetic and copies ran while one was open for 11% -> 9% of each run, Pallas kernels for 12% -> 13%
where the time goes in v1:
time: 260 us; the launch traced here: 258 us
  waiting for transfers between devices  113 us (43%)
  starting transfers between devices  60.9 us (23%)
  Pallas kernels  46.7 us (18%)
  local copies, waits for them, and re-layouts  20.5 us (8%)
  other arithmetic  15.3 us (6%)
    ppermute x35, waiting for transfers between devices, dp_swap(): return lax.ppermute(value, 'dp', [(i, i ^ bit) for i in range(size)])  95.4 us
    pallas_call x16, Pallas kernels, call(): pl.pallas_call(kernel, out_shape=outs, in_specs=[pl.BlockSpec(memory_spac...  46.7 us
    ppermute x35, starting transfers between devices, dp_swap(): return lax.ppermute(value, 'dp', [(i, i ^ bit) for i in range(size)])  46.3 us
    ppermute x23, waiting for transfers between devices, swap(): return lax.ppermute(value, axis, [(0, 1), (1, 0)])  17.7 us
    ppermute x23, starting transfers between devices, swap(): return lax.ppermute(value, axis, [(0, 1), (1, 0)])  14.6 us
    unnamed x96, local copies, waits for them, and re-layouts  12.5 us
  transfers between devices with their start and end apart: 58, of which 22 were waited for; matrix products, arithmetic and copies ran while one was open for 9% of the time, Pallas kernels for 13%

profile of v1, /device:TPU:0, one launch (start us, length us, event | category | flops | bytes accessed | tf_op | source)
XLA Modules:
  0.0 258.0 jit_solution(17619384169880657602)
XLA Ops:
  14.1 4.7 %collective-permute-done.4.got_y = bf16[3,256,256]{2,1,0:T(8,128)(2,1)} collective-permute-done((bf16[3,256,256]{2,1,0:T(8,128)(2,1)}, bf16[3,256,256]{2,1,0:T(8,128)(2,1)}, u32[]{:S(2)}, u32[]{:S(2)}) %collective-permute-start.4) | collective-permute-done | bytes 393248 | tf_op jit(solution)/shard_map/ppermute | solution.py:29
  30.6 3.7 %collective-permute-done.5.got_n = bf16[3,256,256]{2,1,0:T(8,128)(2,1)} collective-permute-done((bf16[3,256,256]{2,1,0:T(8,128)(2,1)}, bf16[3,256,256]{2,1,0:T(8,128)(2,1)}, u32[]{:S(2)}, u32[]{:S(2)}) %collective-permute-start.5) | collective-permute-done | bytes 393248 | tf_op jit(solution)/shard_map/ppermute | solution.py:34
  36.2 6.1 %shard_map.153 = (bf16[512,768]{1,0:T(8,128)(2,1)S(1)}, bf16[512,256]{1,0:T(8,128)(2,1)S(1)}, bf16[4,512,512]{2,1,0:T(8,128)(2,1)S(1)}) custom-call(s32[10]{0:T(128)S(1)} %concatenate.62.ids, bf16[512,1024]{1,0:T(8,128)(2,1)S(1)} %get-tuple-element.99.normed, bf16[2,3,256,512]{3,2,1,0:T(8,128)(2,1)S(1)} %bitcast.102, ...), custom_call_target="tpu_custom_call" | custom-call | flops 1024 | bytes 1024 | tf_op jit(solution)/shard_map/pallas_call | solution.py:58
  50.7 10.3 %collective-permute-done.11 = bf16[512,512]{1,0:T(8,128)(2,1)S(1)} collective-permute-done((bf16[512,512]{1,0:T(8,128)(2,1)S(1)}, bf16[512,512]{1,0:T(8,128)(2,1)S(1)}, u32[]{:S(2)}, u32[]{:S(2)}) %collective-permute-start.11) | collective-permute-done | bytes 524320 | tf_op jit(solution)/shard_map/ppermute | solution.py:29
  61.3 5.3 %collective-permute-done.13.got_n = bf16[2,656,256]{2,1,0:T(8,128)(2,1)S(1)} collective-permute-done((bf16[2,656,256]{2,1,0:T(8,128)(2,1)}, bf16[2,656,256]{2,1,0:T(8,128)(2,1)S(1)}, u32[]{:S(2)}, u32[]{:S(2)}) %collective-permute-start.13) | collective-permute-done | bytes 671776 | tf_op jit(solution)/shard_map/ppermute | solution.py:34
  66.6 5.0 %shard_map.155 = (f32[512,1024]{1,0:T(8,128)S(1)}, bf16[512,1024]{1,0:T(8,128)(2,1)S(1)}, bf16[512,768]{1,0:T(8,128)(2,1)S(1)}, bf16[2,512,656]{2,1,0:T(8,128)(2,1)S(1)}) custom-call(s32[10]{0:T(128)S(1)} %concatenate.62.ids, bf16[512,1024]{1,0:T(8,128)(2,1)S(1)} %get-tuple-element.98.hidden, bf16[512,512]{1,0:T(8,128)(2,1)S(1)} %add_convert_fusion.4.br_own, ...), custom_call_target="tpu_custom_call" | custom-call | flops 1024 | bytes 1024 | tf_op jit(solution)/shard_map/pallas_call | solution.py:58
  71.7 3.6 %shard_map.156 = (f32[512,512]{1,0:T(8,128)S(1)}, bf16[512,512]{1,0:T(8,128)(2,1)S(1)}) custom-call(s32[10]{0:T(128)S(1)} %concatenate.62.ids, bf16[2,512,656]{2,1,0:T(8,128)(2,1)S(1)} %get-tuple-element.119.mix, bf16[2,2,1312,256]{3,2,1,0:T(8,128)(2,1)S(1)} %bitcast.98, bf16[2,656,256]{2,1,0:T(8,128)(2,1)} %collective-permute-done.8.got_y, ...), custom_call_target="tpu_custom_call" | custom-call | flops 1024 | bytes 1024 | tf_op jit(solution)/shard_map/pallas_call | solution.py:58
  85.5 10.8 %collective-permute-done.19 = bf16[4,336,256]{2,1,0:T(8,128)(2,1)S(1)} collective-permute-done((bf16[4,336,256]{2,1,0:T(8,128)(2,1)S(1)}, bf16[4,336,256]{2,1,0:T(8,128)(2,1)S(1)}, u32[]{:S(2)}, u32[]{:S(2)}) %collective-permute-start.19) | collective-permute-done | bytes 688160 | tf_op jit(solution)/shard_map/ppermute | solution.py:34
  108.5 3.5 %shard_map.159 = (f32[512,1024]{1,0:T(8,128)S(1)}, bf16[512,512]{1,0:T(8,128)(2,1)S(1)}, bf16[512,256]{1,0:T(8,128)(2,1)S(1)}, f32[1,1024]{1,0:T(1,128)S(1)}) custom-call(s32[10]{0:T(128)S(1)} %concatenate.62.ids, bf16[512,512]{1,0:T(8,128)(2,1)} %add_convert_fusion.2.g_own, bf16[512,512]{1,0:T(8,128)(2,1)} %collective-permute-done.20.g_got, ...), custom_call_target="tpu_custom_call" | custom-call | flops 1024 | bytes 1024 | tf_op jit(solution)/shard_map/pallas_call | solution.py:58
  112.1 4.2 %shard_map.160.proj.grad = bf16[512,768]{1,0:T(8,128)(2,1)S(1)} custom-call(s32[10]{0:T(128)S(1)} %concatenate.62.ids, bf16[512,768]{1,0:T(8,128)(2,1)S(1)} %copy-done.33, bf16[4,512,512]{2,1,0:T(8,128)(2,1)S(1)} %copy-done.23, bf16[512,256]{1,0:T(8,128)(2,1)S(1)} %get-tuple-element.129.grad, f32[512,128]{1,0:T(8,128)S(1)} %copy-done.19, ...), custom_call_target="tpu_custom_call" | custom-call | flops 1024 | bytes 1024 | tf_op jit(solution)/shard_map/pallas_call | solution.py:58
  127.1 4.3 %collective-permute-start.23 = (bf16[4,64,768]{2,1,0:T(8,128)(2,1)S(1)}, bf16[4,64,768]{2,1,0:T(8,128)(2,1)S(1)}, u32[]{:S(2)}, u32[]{:S(2)}) collective-permute-start(bf16[4,64,768]{2,1,0:T(8,128)(2,1)S(1)} %get-tuple-element.137), channel_id=1, source_target_pairs={{0,4},{4,0},{8,12},{12,8},{16,20},{20,16},{24,28},{28,24},{1,5},{5... | collective-permute-start | bytes 1179656 | tf_op jit(solution)/shard_map/ppermute | solution.py:34
  134.5 8.8 %collective-permute-done.23 = bf16[4,64,768]{2,1,0:T(8,128)(2,1)S(1)} collective-permute-done((bf16[4,64,768]{2,1,0:T(8,128)(2,1)S(1)}, bf16[4,64,768]{2,1,0:T(8,128)(2,1)S(1)}, u32[]{:S(2)}, u32[]{:S(2)}) %collective-permute-start.23) | collective-permute-done | bytes 393248 | tf_op jit(solution)/shard_map/ppermute | solution.py:34
  157.1 6.6 %collective-permute-done.28 = bf16[2,64,1280]{2,1,0:T(8,128)(2,1)S(1)} collective-permute-done((bf16[2,64,1280]{2,1,0:T(8,128)(2,1)S(1)}, bf16[2,64,1280]{2,1,0:T(8,128)(2,1)S(1)}, u32[]{:S(2)}, u32[]{:S(2)}) %collective-permute-start.28) | collective-permute-done | bytes 327712 | tf_op jit(solution)/shard_map/ppermute | solution.py:34
  167.4 11.2 %collective-permute-done.38 = bf16[1,336,256]{2,1,0:T(8,128)(2,1)S(1)} collective-permute-done((bf16[1,336,256]{2,1,0:T(8,128)(2,1)S(1)}, bf16[1,336,256]{2,1,0:T(8,128)(2,1)S(1)}, u32[]{:S(2)}, u32[]{:S(2)}) %collective-permute-start.38) | collective-permute-done | bytes 172064 | tf_op jit(solution)/shard_map/ppermute | solution.py:34
  179.2 3.1 %collective-permute-done.37 = bf16[1,336,256]{2,1,0:T(8,128)(2,1)S(1)} collective-permute-done((bf16[1,336,256]{2,1,0:T(8,128)(2,1)S(1)}, bf16[1,336,256]{2,1,0:T(8,128)(2,1)S(1)}, u32[]{:S(2)}, u32[]{:S(2)}) %collective-permute-start.37) | collective-permute-done | bytes 172064 | tf_op jit(solution)/shard_map/ppermute | solution.py:34
  190.6 3.0 %shard_map.164 = (f32[1024,128]{1,0:T(8,128)}, f32[1,1024]{1,0:T(1,128)S(1)}) custom-call(s32[10]{0:T(128)S(1)} %concatenate.62.ids, bf16[512,512]{1,0:T(8,128)(2,1)S(1)} %add_convert_fusion.g_own, bf16[512,512]{1,0:T(8,128)(2,1)S(1)} %collective-permute-done.34.g_got, bf16[512,1024]{1,0:T(8,128)(2,1)S(1)} %copy-done.7, ...), custom_call_target="tpu_custom_call" | custom-call | flops 1024 | bytes 1024 | tf_op jit(solution)/shard_map/pallas_call | solution.py:58
  194.6 6.5 %collective-permute-done.41 = bf16[1,64,1280]{2,1,0:T(8,128)(2,1)S(1)} collective-permute-done((bf16[1,64,1280]{2,1,0:T(8,128)(2,1)S(1)}, bf16[1,64,1280]{2,1,0:T(8,128)(2,1)S(1)}, u32[]{:S(2)}, u32[]{:S(2)}) %collective-permute-start.41) | collective-permute-done | bytes 163872 | tf_op jit(solution)/shard_map/ppermute | solution.py:34
  204.5 5.5 %collective-permute-done.45 = bf16[1,336,256]{2,1,0:T(8,128)(2,1)S(1)} collective-permute-done((bf16[1,336,256]{2,1,0:T(8,128)(2,1)S(1)}, bf16[1,336,256]{2,1,0:T(8,128)(2,1)S(1)}, u32[]{:S(2)}, u32[]{:S(2)}) %collective-permute-start.45) | collective-permute-done | bytes 172064 | tf_op jit(solution)/shard_map/ppermute | solution.py:34
  210.0 4.9 %collective-permute-done.44 = f32[2,256]{1,0:T(2,128)S(1)} collective-permute-done((f32[2,256]{1,0:T(2,128)S(1)}, f32[2,256]{1,0:T(2,128)S(1)}, u32[]{:S(2)}, u32[]{:S(2)}) %collective-permute-start.44) | collective-permute-done | bytes 2080 | tf_op jit(solution)/shard_map/ppermute | solution.py:34
  222.0 3.5 %collective-permute-done.56 = bf16[2,64,768]{2,1,0:T(8,128)(2,1)S(1)} collective-permute-done((bf16[2,64,768]{2,1,0:T(8,128)(2,1)S(1)}, bf16[2,64,768]{2,1,0:T(8,128)(2,1)S(1)}, u32[]{:S(2)}, u32[]{:S(2)}) %collective-permute-start.56) | collective-permute-done | bytes 196640 | tf_op jit(solution)/shard_map/ppermute | solution.py:34
  228.9 11.7 %collective-permute-done.52 = bf16[2,336,256]{2,1,0:T(8,128)(2,1)S(1)} collective-permute-done((bf16[2,336,256]{2,1,0:T(8,128)(2,1)S(1)}, bf16[2,336,256]{2,1,0:T(8,128)(2,1)S(1)}, u32[]{:S(2)}, u32[]{:S(2)}) %collective-permute-start.52) | collective-permute-done | bytes 344096 | tf_op jit(solution)/shard_map/ppermute | solution.py:34
  240.8 5.3 %collective-permute-done.57.far_second = bf16[4,64,768]{2,1,0:T(8,128)(2,1)S(1)} collective-permute-done((bf16[4,64,768]{2,1,0:T(8,128)(2,1)S(1)}, bf16[4,64,768]{2,1,0:T(8,128)(2,1)S(1)}, u32[]{:S(2)}, u32[]{:S(2)}) %collective-permute-start.57) | collective-permute-done | bytes 393248 | tf_op jit(solution)/shard_map/ppermute | solution.py:34
  248.6 3.1 %collective-permute-done.54.far_second = bf16[4,336,256]{2,1,0:T(8,128)(2,1)S(1)} collective-permute-done((bf16[4,336,256]{2,1,0:T(8,128)(2,1)S(1)}, bf16[4,336,256]{2,1,0:T(8,128)(2,1)S(1)}, u32[]{:S(2)}, u32[]{:S(2)}) %collective-permute-start.54) | collective-permute-done | bytes 688160 | tf_op jit(solution)/shard_map/ppermute | solution.py:34
  251.7 3.4 %shard_map.166 = f32[2,2,1312,256]{3,2,1,0:T(8,128)} custom-call(s32[10]{0:T(128)S(1)} %concatenate.62.ids, bf16[4,336,256]{2,1,0:T(8,128)(2,1)S(1)} %pad_maximum_fusion.own_first, bf16[4,336,256]{2,1,0:T(8,128)(2,1)S(1)} %collective-permute-done.51.own_second, bf16[4,336,256]{2,1,0:T(8,128)(2,1)S(1)} %constant_dynamic-update-slice_fusion.4.far_first, ...), custom_call_target="tpu_custom_call" | custom-call | flops 8000000000 | bytes 1024 | tf_op jit(solution)/shard_map/pallas_call | solution.py:58
  (260 shorter events, 118.3 us)
Async XLA Ops:
  7.5 23.1 %collective-permute-start.6 = (bf16[656,512]{1,0:T(8,128)(2,1)}, bf16[656,512]{1,0:T(8,128)(2,1)}, u32[]{:S(2)}, u32[]{:S(2)}) collective-permute-start(bf16[656,512]{1,0:T(8,128)(2,1)} %dynamic-slice_bitcast_fusion), channel_id=1, source_target_pairs={{0,2},{2,0},{1,3},{3,1},{4,6},{6,4},{5,7},{7,5},{8,10},{10,8},{9,1... | collective-permute-start | bytes 2015240 | tf_op jit(solution)/shard_map/ppermute | solution.py:29
  18.8 25.7 %collective-permute-start.8 = (bf16[2,656,256]{2,1,0:T(8,128)(2,1)}, bf16[2,656,256]{2,1,0:T(8,128)(2,1)}, u32[]{:S(2)}, u32[]{:S(2)}) collective-permute-start(bf16[2,656,256]{2,1,0:T(8,128)(2,1)} %dynamic-slice_bitcast_fusion.1), channel_id=1, source_target_pairs={{0,1},{1,0},{2,3},{3,2},{4,5},{5,4},{6,7},{7,6},{8,9},{9,8},{10,11... | collective-permute-start | bytes 2015240 | tf_op jit(solution)/shard_map/ppermute | solution.py:29
  25.9 18.6 %collective-permute-start.9 = (bf16[512,256]{1,0:T(8,128)(2,1)}, bf16[512,256]{1,0:T(8,128)(2,1)S(1)}, u32[]{:S(2)}, u32[]{:S(2)}) collective-permute-start(bf16[512,256]{1,0:T(8,128)(2,1)} %bitcast.112), channel_id=1, source_target_pairs={{0,1},{1,0},{2,3},{3,2},{4,5},{5,4},{6,7},{7,6},{8,9},{9,8},{10,11... | collective-permute-start | bytes 786440 | tf_op jit(solution)/shard_map/ppermute | solution.py:29
  48.9 17.7 %collective-permute-start.13 = (bf16[2,656,256]{2,1,0:T(8,128)(2,1)}, bf16[2,656,256]{2,1,0:T(8,128)(2,1)S(1)}, u32[]{:S(2)}, u32[]{:S(2)}) collective-permute-start(bf16[2,656,256]{2,1,0:T(8,128)(2,1)} %collective-permute-done.8.got_y), channel_id=1, source_target_pairs={{0,4},{4,0},{8,12},{12,8},{16,20},{20,16},{24,28},{28,24},{1,5},{5... | collective-permute-start | bytes 2015240 | tf_op jit(solution)/shard_map/ppermute | solution.py:34
  101.5 20.9 %collective-permute-start.26 = (bf16[2,336,256]{2,1,0:T(8,128)(2,1)}, bf16[2,336,256]{2,1,0:T(8,128)(2,1)}, u32[]{:S(2)}, u32[]{:S(2)}) collective-permute-start(bf16[2,336,256]{2,1,0:T(8,128)(2,1)} %get-tuple-element.213), channel_id=1, source_target_pairs={{0,4},{4,0},{8,12},{12,8},{16,20},{20,16},{24,28},{28,24},{1,5},{5... | collective-permute-start | bytes 1032200 | tf_op jit(solution)/shard_map/ppermute | solution.py:34
  101.8 30.6 %collective-permute-start.24 = (bf16[4,336,256]{2,1,0:T(8,128)(2,1)}, bf16[4,336,256]{2,1,0:T(8,128)(2,1)}, u32[]{:S(2)}, u32[]{:S(2)}) collective-permute-start(bf16[4,336,256]{2,1,0:T(8,128)(2,1)} %bitcast.36), channel_id=1, source_target_pairs={{0,8},{4,12},{8,0},{12,4},{16,24},{20,28},{24,16},{28,20},{1,9},{5... | collective-permute-start | bytes 2064392 | tf_op jit(solution)/shard_map/ppermute | solution.py:34
  103.5 23.5 %collective-permute-start.25 = (bf16[2,336,256]{2,1,0:T(8,128)(2,1)}, bf16[2,336,256]{2,1,0:T(8,128)(2,1)}, u32[]{:S(2)}, u32[]{:S(2)}) collective-permute-start(bf16[2,336,256]{2,1,0:T(8,128)(2,1)} %get-tuple-element.211), channel_id=1, source_target_pairs={{0,8},{4,12},{8,0},{12,4},{16,24},{20,28},{24,16},{28,20},{1,9},{5... | collective-permute-start | bytes 1032200 | tf_op jit(solution)/shard_map/ppermute | solution.py:34
  118.2 26.6 %collective-permute-start.22 = (bf16[4,64,1280]{2,1,0:T(8,128)(2,1)S(1)}, bf16[4,64,1280]{2,1,0:T(8,128)(2,1)S(1)}, u32[]{:S(2)}, u32[]{:S(2)}) collective-permute-start(bf16[4,64,1280]{2,1,0:T(8,128)(2,1)S(1)} %get-tuple-element.131), channel_id=1, source_target_pairs={{0,4},{4,0},{8,12},{12,8},{16,20},{20,16},{24,28},{28,24},{1,5},{5... | collective-permute-start | bytes 1966088 | tf_op jit(solution)/shard_map/ppermute | solution.py:34
  122.3 24.4 %collective-permute-start.21 = (bf16[512,512]{1,0:T(8,128)(2,1)S(1)}, bf16[512,512]{1,0:T(8,128)(2,1)S(1)}, u32[]{:S(2)}, u32[]{:S(2)}) collective-permute-start(bf16[512,512]{1,0:T(8,128)(2,1)S(1)} %get-tuple-element.134), channel_id=1, source_target_pairs={{0,2},{2,0},{1,3},{3,1},{4,6},{6,4},{5,7},{7,5},{8,10},{10,8},{9,1... | collective-permute-start | bytes 1572872 | tf_op jit(solution)/shard_map/ppermute | solution.py:29
  123.5 23.9 %collective-permute-start.32 = (bf16[1,336,256]{2,1,0:T(8,128)(2,1)S(1)}, bf16[1,336,256]{2,1,0:T(8,128)(2,1)S(1)}, u32[]{:S(2)}, u32[]{:S(2)}) collective-permute-start(bf16[1,336,256]{2,1,0:T(8,128)(2,1)S(1)} %broadcast_select_fusion.12), channel_id=1, source_target_pairs={{0,16},{4,20},{8,24},{12,28},{16,0},{20,4},{24,8},{28,12},{1,17},{... | collective-permute-start | bytes 516104 | tf_op jit(solution)/shard_map/ppermute | solution.py:34
  132.4 17.7 %collective-permute-start.31 = (bf16[1,336,256]{2,1,0:T(8,128)(2,1)S(1)}, bf16[1,336,256]{2,1,0:T(8,128)(2,1)S(1)}, u32[]{:S(2)}, u32[]{:S(2)}) collective-permute-start(bf16[1,336,256]{2,1,0:T(8,128)(2,1)S(1)} %broadcast_select_fusion.11), channel_id=1, source_target_pairs={{0,16},{4,20},{8,24},{12,28},{16,0},{20,4},{24,8},{28,12},{1,17},{... | collective-permute-start | bytes 516104 | tf_op jit(solution)/shard_map/ppermute | solution.py:34
  153.9 24.6 %collective-permute-start.38 = (bf16[1,336,256]{2,1,0:T(8,128)(2,1)S(1)}, bf16[1,336,256]{2,1,0:T(8,128)(2,1)S(1)}, u32[]{:S(2)}, u32[]{:S(2)}) collective-permute-start(bf16[1,336,256]{2,1,0:T(8,128)(2,1)S(1)} %add_convert_fusion.13), channel_id=1, source_target_pairs={{0,16},{4,20},{8,24},{12,28},{16,0},{20,4},{24,8},{28,12},{1,17},{... | collective-permute-start | bytes 516104 | tf_op jit(solution)/shard_map/ppermute | solution.py:34
  155.0 27.3 %collective-permute-start.37 = (bf16[1,336,256]{2,1,0:T(8,128)(2,1)S(1)}, bf16[1,336,256]{2,1,0:T(8,128)(2,1)S(1)}, u32[]{:S(2)}, u32[]{:S(2)}) collective-permute-start(bf16[1,336,256]{2,1,0:T(8,128)(2,1)S(1)} %broadcast_select_fusion.10), channel_id=1, source_target_pairs={{0,16},{4,20},{8,24},{12,28},{16,0},{20,4},{24,8},{28,12},{1,17},{... | collective-permute-start | bytes 516104 | tf_op jit(solution)/shard_map/ppermute | solution.py:34
  163.8 20.7 %collective-permute-start.36 = (bf16[1,64,768]{2,1,0:T(8,128)(2,1)S(1)}, bf16[1,64,768]{2,1,0:T(8,128)(2,1)S(1)}, u32[]{:S(2)}, u32[]{:S(2)}) collective-permute-start(bf16[1,64,768]{2,1,0:T(8,128)(2,1)S(1)} %broadcast_select_fusion.14), channel_id=1, source_target_pairs={{0,16},{4,20},{8,24},{12,28},{16,0},{20,4},{24,8},{28,12},{1,17},{... | collective-permute-start | bytes 294920 | tf_op jit(solution)/shard_map/ppermute | solution.py:34
  164.3 22.3 %collective-permute-start.35 = (bf16[1,64,1280]{2,1,0:T(8,128)(2,1)S(1)}, bf16[1,64,1280]{2,1,0:T(8,128)(2,1)S(1)}, u32[]{:S(2)}, u32[]{:S(2)}) collective-permute-start(bf16[1,64,1280]{2,1,0:T(8,128)(2,1)S(1)} %broadcast_select_fusion.13), channel_id=1, source_target_pairs={{0,16},{4,20},{8,24},{12,28},{16,0},{20,4},{24,8},{28,12},{1,17},{... | collective-permute-start | bytes 491528 | tf_op jit(solution)/shard_map/ppermute | solution.py:34
  167.3 21.0 %collective-permute-start.34 = (bf16[512,512]{1,0:T(8,128)(2,1)S(1)}, bf16[512,512]{1,0:T(8,128)(2,1)S(1)}, u32[]{:S(2)}, u32[]{:S(2)}) collective-permute-start(bf16[512,512]{1,0:T(8,128)(2,1)S(1)} %add_convert_fusion.g_own), channel_id=1, source_target_pairs={{0,2},{2,0},{1,3},{3,1},{4,6},{6,4},{5,7},{7,5},{8,10},{10,8},{9,1... | collective-permute-start | bytes 1572872 | tf_op jit(solution)/shard_map/ppermute | solution.py:29
  178.6 43.1 %collective-permute-start.53 = (bf16[2,336,256]{2,1,0:T(8,128)(2,1)S(1)}, bf16[2,336,256]{2,1,0:T(8,128)(2,1)S(1)}, u32[]{:S(2)}, u32[]{:S(2)}) collective-permute-start(bf16[2,336,256]{2,1,0:T(8,128)(2,1)S(1)} %pad_maximum_fusion.4), channel_id=1, source_target_pairs={{0,4},{4,0},{8,12},{12,8},{16,20},{20,16},{24,28},{28,24},{1,5},{5... | collective-permute-start | bytes 1032200 | tf_op jit(solution)/shard_map/ppermute | solution.py:34
  182.3 21.9 %collective-permute-start.46 = (bf16[2,336,256]{2,1,0:T(8,128)(2,1)S(1)}, bf16[2,336,256]{2,1,0:T(8,128)(2,1)S(1)}, u32[]{:S(2)}, u32[]{:S(2)}) collective-permute-start(bf16[2,336,256]{2,1,0:T(8,128)(2,1)S(1)} %pad_maximum_fusion.5), channel_id=1, source_target_pairs={{0,8},{4,12},{8,0},{12,4},{16,24},{20,28},{24,16},{28,20},{1,9},{5... | collective-permute-start | bytes 1032200 | tf_op jit(solution)/shard_map/ppermute | solution.py:34
  193.7 32.5 %collective-permute-start.33 = (bf16[512,256]{1,0:T(8,128)(2,1)S(1)}, bf16[512,256]{1,0:T(8,128)(2,1)S(1)}, u32[]{:S(2)}, u32[]{:S(2)}) collective-permute-start(bf16[512,256]{1,0:T(8,128)(2,1)S(1)} %get-tuple-element.153), channel_id=1, source_target_pairs={{0,1},{1,0},{2,3},{3,2},{4,5},{5,4},{6,7},{7,6},{8,9},{9,8},{10,11... | collective-permute-start | bytes 786440 | tf_op jit(solution)/shard_map/ppermute | solution.py:29
  214.9 25.9 %collective-permute-start.51 = (bf16[4,336,256]{2,1,0:T(8,128)(2,1)S(1)}, bf16[4,336,256]{2,1,0:T(8,128)(2,1)S(1)}, u32[]{:S(2)}, u32[]{:S(2)}) collective-permute-start(bf16[4,336,256]{2,1,0:T(8,128)(2,1)S(1)} %pad_maximum_fusion.own_first), channel_id=1, source_target_pairs={{0,4},{4,0},{8,12},{12,8},{16,20},{20,16},{24,28},{28,24},{1,5},{5... | collective-permute-start | bytes 2064392 | tf_op jit(solution)/shard_map/ppermute | solution.py:34
  220.8 19.8 %collective-permute-start.52 = (bf16[2,336,256]{2,1,0:T(8,128)(2,1)S(1)}, bf16[2,336,256]{2,1,0:T(8,128)(2,1)S(1)}, u32[]{:S(2)}, u32[]{:S(2)}) collective-permute-start(bf16[2,336,256]{2,1,0:T(8,128)(2,1)S(1)} %get-tuple-element.219), channel_id=1, source_target_pairs={{0,4},{4,0},{8,12},{12,8},{16,20},{20,16},{24,28},{28,24},{1,5},{5... | collective-permute-start | bytes 1032200 | tf_op jit(solution)/shard_map/ppermute | solution.py:34
  221.7 24.4 %collective-permute-start.55 = (bf16[4,336,256]{2,1,0:T(8,128)(2,1)S(1)}, bf16[4,336,256]{2,1,0:T(8,128)(2,1)S(1)}, u32[]{:S(2)}, u32[]{:S(2)}) collective-permute-start(bf16[4,336,256]{2,1,0:T(8,128)(2,1)S(1)} %pad_maximum_fusion.1.first), channel_id=1, source_target_pairs={{0,8},{4,12},{8,0},{12,4},{16,24},{20,28},{24,16},{28,20},{1,9},{5... | collective-permute-start | bytes 2064392 | tf_op jit(solution)/shard_map/ppermute | solution.py:34
  225.5 20.6 %collective-permute-start.57 = (bf16[4,64,768]{2,1,0:T(8,128)(2,1)S(1)}, bf16[4,64,768]{2,1,0:T(8,128)(2,1)S(1)}, u32[]{:S(2)}, u32[]{:S(2)}) collective-permute-start(bf16[4,64,768]{2,1,0:T(8,128)(2,1)S(1)} %constant_dynamic-update-slice_fusion.7.far_first), channel_id=1, source_target_pairs={{0,4},{4,0},{8,12},{12,8},{16,20},{20,16},{24,28},{28,24},{1,5},{5... | collective-permute-start | bytes 1179656 | tf_op jit(solution)/shard_map/ppermute | solution.py:34
  227.0 28.1 %collective-permute-start.50 = (bf16[4,64,1280]{2,1,0:T(8,128)(2,1)S(1)}, bf16[4,64,1280]{2,1,0:T(8,128)(2,1)S(1)}, u32[]{:S(2)}, u32[]{:S(2)}) collective-permute-start(bf16[4,64,1280]{2,1,0:T(8,128)(2,1)S(1)} %pad_maximum_fusion.2.own_first), channel_id=1, source_target_pairs={{0,4},{4,0},{8,12},{12,8},{16,20},{20,16},{24,28},{28,24},{1,5},{5... | collective-permute-start | bytes 1966088 | tf_op jit(solution)/shard_map/ppermute | solution.py:34
  (80 other events, 789.9 us)

commit v2 on v1

--- a/solution.py
+++ b/solution.py
@@ -14,7 +14,7 @@
 F32 = jnp.float32
 BF = jnp.bfloat16
 LATE = (
-    "W2", "L2", "L1", "G", "W1", "W2", "G", "L2", "L1", "G", "O", "W2", "W1", "L2",
+    "W1", "W2", "L2", "L1", "G", "W2", "W1", "G", "L2", "L1", "G", "O", "W2", "L2",
 )
 NN = ((1,), (0,))
 NT = ((1,), (1,))
@@ -570,7 +570,9 @@
     w_out = wout.reshape(2, width, half)
     out_got = swap(lax.dynamic_index_in_dim(w_out, 1 - row, 0, False), "row")
 
-    qkv_n, down_got, out_got = lax.optimization_barrier((qkv_n, down_got, out_got))
+    qkv_n, down_got, out_got, occupied = lax.optimization_barrier(
+        (qkv_n, down_got, out_got, occupied)
+    )
 
     grad_x = swap(grad_own, "col")
 

time: 260 us -> 258 us (level)
  local copies, waits for them, and re-layouts: 20.5 us -> 16.6 us
  other arithmetic: 15.3 us -> 18.5 us
    ppermute x35, starting transfers between devices: 46.3 us -> 49.1 us  [dp_swap(): return lax.ppermute(value, 'dp', [(i, i ^ bit) for i in range(size)])]
    unnamed x96 -> x88, local copies, waits for them, and re-layouts: 12.5 us -> 9.85 us
  transfers between devices with their start and end apart: 58 -> 58, of which waited for: 22 -> 24; matrix products, arithmetic and copies ran while one was open for 9% -> 9% of each run, Pallas kernels for 13% -> 14%
where the time goes in v2:
time: 258 us
  waiting for transfers between devices  111 us (43%)
  starting transfers between devices  62.4 us (24%)
  Pallas kernels  48 us (19%)
  other arithmetic  18.5 us (7%)
  local copies, waits for them, and re-layouts  16.6 us (6%)
    ppermute x35, waiting for transfers between devices, dp_swap(): return lax.ppermute(value, 'dp', [(i, i ^ bit) for i in range(size)])  94.5 us
    ppermute x35, starting transfers between devices, dp_swap(): return lax.ppermute(value, 'dp', [(i, i ^ bit) for i in range(size)])  49.1 us
    pallas_call x16, Pallas kernels, call(): pl.pallas_call(kernel, out_shape=outs, in_specs=[pl.BlockSpec(memory_spac...  48 us
    ppermute x23, waiting for transfers between devices, swap(): return lax.ppermute(value, axis, [(0, 1), (1, 0)])  16.3 us
    ppermute x23, starting transfers between devices, swap(): return lax.ppermute(value, axis, [(0, 1), (1, 0)])  13.2 us
    unnamed x88, local copies, waits for them, and re-layouts  9.85 us
  transfers between devices with their start and end apart: 58, of which 24 were waited for; matrix products, arithmetic and copies ran while one was open for 9% of the time, Pallas kernels for 14%

profile of v2, /device:TPU:0, one launch (start us, length us, event | category | flops | bytes accessed | tf_op | source)
XLA Modules:
  0.0 257.8 jit_solution(9882671193037933075)
XLA Ops:
  8.1 3.1 %collective-permute-done.own_x = bf16[512,256]{1,0:T(8,128)(2,1)} collective-permute-done((bf16[512,256]{1,0:T(8,128)(2,1)}, bf16[512,256]{1,0:T(8,128)(2,1)}, u32[]{:S(2)}, u32[]{:S(2)}) %collective-permute-start) | collective-permute-done | bytes 262176 | tf_op jit(solution)/shard_map/ppermute | solution.py:29
  29.6 4.1 %collective-permute-done.5.got_n = bf16[3,256,256]{2,1,0:T(8,128)(2,1)} collective-permute-done((bf16[3,256,256]{2,1,0:T(8,128)(2,1)}, bf16[3,256,256]{2,1,0:T(8,128)(2,1)}, u32[]{:S(2)}, u32[]{:S(2)}) %collective-permute-start.5) | collective-permute-done | bytes 393248 | tf_op jit(solution)/shard_map/ppermute | solution.py:34
  36.1 6.0 %shard_map.153 = (bf16[512,768]{1,0:T(8,128)(2,1)S(1)}, bf16[512,256]{1,0:T(8,128)(2,1)S(1)}, bf16[4,512,512]{2,1,0:T(8,128)(2,1)S(1)}) custom-call(s32[10]{0:T(128)S(1)} %concatenate.62.ids, bf16[512,1024]{1,0:T(8,128)(2,1)S(1)} %get-tuple-element.100.normed, bf16[2,3,256,512]{3,2,1,0:T(8,128)(2,1)S(1)} %bitcast.102, ...), custom_call_target="tpu_custom_call" | custom-call | flops 1024 | bytes 1024 | tf_op jit(solution)/shard_map/pallas_call | solution.py:58
  50.6 10.5 %collective-permute-done.11 = bf16[512,512]{1,0:T(8,128)(2,1)} collective-permute-done((bf16[512,512]{1,0:T(8,128)(2,1)}, bf16[512,512]{1,0:T(8,128)(2,1)}, u32[]{:S(2)}, u32[]{:S(2)}) %collective-permute-start.11) | collective-permute-done | bytes 524320 | tf_op jit(solution)/shard_map/ppermute | solution.py:29
  62.6 3.9 %collective-permute-done.13.got_n = bf16[2,656,256]{2,1,0:T(8,128)(2,1)S(1)} collective-permute-done((bf16[2,656,256]{2,1,0:T(8,128)(2,1)}, bf16[2,656,256]{2,1,0:T(8,128)(2,1)S(1)}, u32[]{:S(2)}, u32[]{:S(2)}) %collective-permute-start.13) | collective-permute-done | bytes 671776 | tf_op jit(solution)/shard_map/ppermute | solution.py:34
  66.5 5.1 %shard_map.155 = (f32[512,1024]{1,0:T(8,128)S(1)}, bf16[512,1024]{1,0:T(8,128)(2,1)S(1)}, bf16[512,768]{1,0:T(8,128)(2,1)S(1)}, bf16[2,512,656]{2,1,0:T(8,128)(2,1)S(1)}) custom-call(s32[10]{0:T(128)S(1)} %concatenate.62.ids, bf16[512,1024]{1,0:T(8,128)(2,1)S(1)} %copy-done.8, bf16[512,512]{1,0:T(8,128)(2,1)S(1)} %add_convert_fusion.4.br_own, ...), custom_call_target="tpu_custom_call" | custom-call | flops 1024 | bytes 1024 | tf_op jit(solution)/shard_map/pallas_call | solution.py:58
  73.0 3.3 %shard_map.156 = (f32[512,512]{1,0:T(8,128)S(1)}, bf16[512,512]{1,0:T(8,128)(2,1)S(1)}) custom-call(s32[10]{0:T(128)S(1)} %concatenate.62.ids, bf16[2,512,656]{2,1,0:T(8,128)(2,1)S(1)} %get-tuple-element.121.mix, bf16[2,2,1312,256]{3,2,1,0:T(8,128)(2,1)S(1)} %bitcast.98, bf16[2,656,256]{2,1,0:T(8,128)(2,1)} %collective-permute-done.8.got_y, ...), custom_call_target="tpu_custom_call" | custom-call | flops 1024 | bytes 1024 | tf_op jit(solution)/shard_map/pallas_call | solution.py:58
  76.9 3.2 %shard_map.158 = (bf16[2,2,336,256]{3,2,1,0:T(8,128)(2,1)S(1)}, bf16[2,2,336,256]{3,2,1,0:T(8,128)(2,1)S(1)}, bf16[2,2,336,256]{3,2,1,0:T(8,128)(2,1)S(1)}, bf16[2,2,336,256]{3,2,1,0:T(8,128)(2,1)}) custom-call(s32[10]{0:T(128)S(1)} %concatenate.62.ids, bf16[2,512,656]{2,1,0:T(8,128)(2,1)S(1)} %get-tuple-element.121.mix, ...), custom_call_target="tpu_custom_call" | custom-call | flops 1024 | bytes 1024 | tf_op jit(solution)/shard_map/pallas_call | solution.py:58
  86.6 11.0 %collective-permute-done.19 = bf16[4,336,256]{2,1,0:T(8,128)(2,1)S(1)} collective-permute-done((bf16[4,336,256]{2,1,0:T(8,128)(2,1)S(1)}, bf16[4,336,256]{2,1,0:T(8,128)(2,1)S(1)}, u32[]{:S(2)}, u32[]{:S(2)}) %collective-permute-start.19) | collective-permute-done | bytes 688160 | tf_op jit(solution)/shard_map/ppermute | solution.py:34
  107.1 3.5 %shard_map.159 = (f32[512,1024]{1,0:T(8,128)S(1)}, bf16[512,512]{1,0:T(8,128)(2,1)S(1)}, bf16[512,256]{1,0:T(8,128)(2,1)S(1)}, f32[1,1024]{1,0:T(1,128)S(1)}) custom-call(s32[10]{0:T(128)S(1)} %concatenate.62.ids, bf16[512,512]{1,0:T(8,128)(2,1)} %add_convert_fusion.2.g_own, bf16[512,512]{1,0:T(8,128)(2,1)} %collective-permute-done.20.g_got, ...), custom_call_target="tpu_custom_call" | custom-call | flops 1024 | bytes 1024 | tf_op jit(solution)/shard_map/pallas_call | solution.py:58
  110.6 4.2 %shard_map.160.proj.grad = bf16[512,768]{1,0:T(8,128)(2,1)S(1)} custom-call(s32[10]{0:T(128)S(1)} %concatenate.62.ids, bf16[512,768]{1,0:T(8,128)(2,1)S(1)} %copy-done.31, bf16[4,512,512]{2,1,0:T(8,128)(2,1)S(1)} %copy-done.23, bf16[512,256]{1,0:T(8,128)(2,1)S(1)} %get-tuple-element.131.grad, f32[512,128]{1,0:T(8,128)S(1)} %copy-done.19, ...), custom_call_target="tpu_custom_call" | custom-call | flops 1024 | bytes 1024 | tf_op jit(solution)/shard_map/pallas_call | solution.py:58
  124.7 7.2 %collective-permute-done.25 = bf16[2,336,256]{2,1,0:T(8,128)(2,1)} collective-permute-done((bf16[2,336,256]{2,1,0:T(8,128)(2,1)}, bf16[2,336,256]{2,1,0:T(8,128)(2,1)}, u32[]{:S(2)}, u32[]{:S(2)}) %collective-permute-start.25) | collective-permute-done | bytes 344096 | tf_op jit(solution)/shard_map/ppermute | solution.py:34
  137.2 5.1 %collective-permute-done.23 = bf16[4,64,768]{2,1,0:T(8,128)(2,1)S(1)} collective-permute-done((bf16[4,64,768]{2,1,0:T(8,128)(2,1)S(1)}, bf16[4,64,768]{2,1,0:T(8,128)(2,1)S(1)}, u32[]{:S(2)}, u32[]{:S(2)}) %collective-permute-start.23) | collective-permute-done | bytes 393248 | tf_op jit(solution)/shard_map/ppermute | solution.py:34
  156.6 6.1 %collective-permute-done.28 = bf16[2,64,1280]{2,1,0:T(8,128)(2,1)S(1)} collective-permute-done((bf16[2,64,1280]{2,1,0:T(8,128)(2,1)S(1)}, bf16[2,64,1280]{2,1,0:T(8,128)(2,1)S(1)}, u32[]{:S(2)}, u32[]{:S(2)}) %collective-permute-start.28) | collective-permute-done | bytes 327712 | tf_op jit(solution)/shard_map/ppermute | solution.py:34
  166.2 11.9 %collective-permute-done.38 = bf16[1,336,256]{2,1,0:T(8,128)(2,1)S(1)} collective-permute-done((bf16[1,336,256]{2,1,0:T(8,128)(2,1)S(1)}, bf16[1,336,256]{2,1,0:T(8,128)(2,1)S(1)}, u32[]{:S(2)}, u32[]{:S(2)}) %collective-permute-start.38) | collective-permute-done | bytes 172064 | tf_op jit(solution)/shard_map/ppermute | solution.py:34
  178.5 3.3 %collective-permute-done.37 = bf16[1,336,256]{2,1,0:T(8,128)(2,1)S(1)} collective-permute-done((bf16[1,336,256]{2,1,0:T(8,128)(2,1)S(1)}, bf16[1,336,256]{2,1,0:T(8,128)(2,1)S(1)}, u32[]{:S(2)}, u32[]{:S(2)}) %collective-permute-start.37) | collective-permute-done | bytes 172064 | tf_op jit(solution)/shard_map/ppermute | solution.py:34
  192.5 3.6 %collective-permute-done.44 = bf16[2,336,256]{2,1,0:T(8,128)(2,1)S(1)} collective-permute-done((bf16[2,336,256]{2,1,0:T(8,128)(2,1)S(1)}, bf16[2,336,256]{2,1,0:T(8,128)(2,1)S(1)}, u32[]{:S(2)}, u32[]{:S(2)}) %collective-permute-start.44) | collective-permute-done | bytes 344096 | tf_op jit(solution)/shard_map/ppermute | solution.py:34
  206.4 5.1 %collective-permute-done.51 = bf16[1,336,256]{2,1,0:T(8,128)(2,1)S(1)} collective-permute-done((bf16[1,336,256]{2,1,0:T(8,128)(2,1)S(1)}, bf16[1,336,256]{2,1,0:T(8,128)(2,1)S(1)}, u32[]{:S(2)}, u32[]{:S(2)}) %collective-permute-start.51) | collective-permute-done | bytes 172064 | tf_op jit(solution)/shard_map/ppermute | solution.py:34
  211.5 3.4 %collective-permute-start.46 = (f32[2,256]{1,0:T(2,128)S(1)}, f32[2,256]{1,0:T(2,128)S(1)}, u32[]{:S(2)}, u32[]{:S(2)}) collective-permute-start(f32[2,256]{1,0:T(2,128)S(1)} %fusion.11), channel_id=1, source_target_pairs={{0,16},{4,20},{8,24},{12,28},{16,0},{20,4},{24,8},{28,12},{1,17},{... | collective-permute-start | bytes 6152 | tf_op jit(solution)/shard_map/ppermute | solution.py:34
  216.6 4.1 %collective-permute-start.56 = (bf16[2,64,768]{2,1,0:T(8,128)(2,1)S(1)}, bf16[2,64,768]{2,1,0:T(8,128)(2,1)S(1)}, u32[]{:S(2)}, u32[]{:S(2)}) collective-permute-start(bf16[2,64,768]{2,1,0:T(8,128)(2,1)S(1)} %get-tuple-element.225), channel_id=1, source_target_pairs={{0,8},{4,12},{8,0},{12,4},{16,24},{20,28},{24,16},{28,20},{1,9},{5... | collective-permute-start | bytes 589832 | tf_op jit(solution)/shard_map/ppermute | solution.py:34
  220.9 7.8 %collective-permute-done.52 = bf16[2,336,256]{2,1,0:T(8,128)(2,1)S(1)} collective-permute-done((bf16[2,336,256]{2,1,0:T(8,128)(2,1)S(1)}, bf16[2,336,256]{2,1,0:T(8,128)(2,1)S(1)}, u32[]{:S(2)}, u32[]{:S(2)}) %collective-permute-start.52) | collective-permute-done | bytes 344096 | tf_op jit(solution)/shard_map/ppermute | solution.py:34
  234.3 6.6 %collective-permute-done.57.far_second = bf16[4,64,768]{2,1,0:T(8,128)(2,1)S(1)} collective-permute-done((bf16[4,64,768]{2,1,0:T(8,128)(2,1)S(1)}, bf16[4,64,768]{2,1,0:T(8,128)(2,1)S(1)}, u32[]{:S(2)}, u32[]{:S(2)}) %collective-permute-start.57) | collective-permute-done | bytes 393248 | tf_op jit(solution)/shard_map/ppermute | solution.py:34
  243.8 7.7 %collective-permute-done.54.far_second = bf16[4,336,256]{2,1,0:T(8,128)(2,1)S(1)} collective-permute-done((bf16[4,336,256]{2,1,0:T(8,128)(2,1)S(1)}, bf16[4,336,256]{2,1,0:T(8,128)(2,1)S(1)}, u32[]{:S(2)}, u32[]{:S(2)}) %collective-permute-start.54) | collective-permute-done | bytes 688160 | tf_op jit(solution)/shard_map/ppermute | solution.py:34
  251.5 3.4 %shard_map.166 = f32[2,2,1312,256]{3,2,1,0:T(8,128)} custom-call(s32[10]{0:T(128)S(1)} %concatenate.62.ids, bf16[4,336,256]{2,1,0:T(8,128)(2,1)S(1)} %pad_maximum_fusion.own_first, bf16[4,336,256]{2,1,0:T(8,128)(2,1)S(1)} %collective-permute-done.50.own_second, bf16[4,336,256]{2,1,0:T(8,128)(2,1)S(1)} %constant_dynamic-update-slice_fusion.4.far_first, ...), custom_call_target="tpu_custom_call" | custom-call | flops 8000000000 | bytes 1024 | tf_op jit(solution)/shard_map/pallas_call | solution.py:58
  (253 shorter events, 123.1 us)
Async XLA Ops:
  7.7 21.9 %collective-permute-start.6 = (bf16[656,512]{1,0:T(8,128)(2,1)}, bf16[656,512]{1,0:T(8,128)(2,1)}, u32[]{:S(2)}, u32[]{:S(2)}) collective-permute-start(bf16[656,512]{1,0:T(8,128)(2,1)} %dynamic-slice_bitcast_fusion), channel_id=1, source_target_pairs={{0,2},{2,0},{1,3},{3,1},{4,6},{6,4},{5,7},{7,5},{8,10},{10,8},{9,1... | collective-permute-start | bytes 2015240 | tf_op jit(solution)/shard_map/ppermute | solution.py:29
  18.7 24.7 %collective-permute-start.8 = (bf16[2,656,256]{2,1,0:T(8,128)(2,1)}, bf16[2,656,256]{2,1,0:T(8,128)(2,1)}, u32[]{:S(2)}, u32[]{:S(2)}) collective-permute-start(bf16[2,656,256]{2,1,0:T(8,128)(2,1)} %dynamic-slice_bitcast_fusion.1), channel_id=1, source_target_pairs={{0,1},{1,0},{2,3},{3,2},{4,5},{5,4},{6,7},{7,6},{8,9},{9,8},{10,11... | collective-permute-start | bytes 2015240 | tf_op jit(solution)/shard_map/ppermute | solution.py:29
  24.4 19.0 %collective-permute-start.9 = (bf16[512,256]{1,0:T(8,128)(2,1)}, bf16[512,256]{1,0:T(8,128)(2,1)S(1)}, u32[]{:S(2)}, u32[]{:S(2)}) collective-permute-start(bf16[512,256]{1,0:T(8,128)(2,1)} %bitcast.111), channel_id=1, source_target_pairs={{0,1},{1,0},{2,3},{3,2},{4,5},{5,4},{6,7},{7,6},{8,9},{9,8},{10,11... | collective-permute-start | bytes 786440 | tf_op jit(solution)/shard_map/ppermute | solution.py:29
  48.8 17.7 %collective-permute-start.13 = (bf16[2,656,256]{2,1,0:T(8,128)(2,1)}, bf16[2,656,256]{2,1,0:T(8,128)(2,1)S(1)}, u32[]{:S(2)}, u32[]{:S(2)}) collective-permute-start(bf16[2,656,256]{2,1,0:T(8,128)(2,1)} %collective-permute-done.8.got_y), channel_id=1, source_target_pairs={{0,4},{4,0},{8,12},{12,8},{16,20},{20,16},{24,28},{28,24},{1,5},{5... | collective-permute-start | bytes 2015240 | tf_op jit(solution)/shard_map/ppermute | solution.py:34
  80.1 17.4 %collective-permute-start.19 = (bf16[4,336,256]{2,1,0:T(8,128)(2,1)S(1)}, bf16[4,336,256]{2,1,0:T(8,128)(2,1)S(1)}, u32[]{:S(2)}, u32[]{:S(2)}) collective-permute-start(bf16[4,336,256]{2,1,0:T(8,128)(2,1)S(1)} %bitcast.109), channel_id=1, source_target_pairs={{0,4},{4,0},{8,12},{12,8},{16,20},{20,16},{24,28},{28,24},{1,5},{5... | collective-permute-start | bytes 2064392 | tf_op jit(solution)/shard_map/ppermute | solution.py:34
  83.5 17.2 %collective-permute-start.18 = (bf16[4,336,256]{2,1,0:T(8,128)(2,1)S(1)}, bf16[4,336,256]{2,1,0:T(8,128)(2,1)S(1)}, u32[]{:S(2)}, u32[]{:S(2)}) collective-permute-start(bf16[4,336,256]{2,1,0:T(8,128)(2,1)S(1)} %bitcast.110), channel_id=1, source_target_pairs={{0,8},{4,12},{8,0},{12,4},{16,24},{20,28},{24,16},{28,20},{1,9},{5... | collective-permute-start | bytes 2064392 | tf_op jit(solution)/shard_map/ppermute | solution.py:34
  102.7 18.3 %collective-permute-start.26 = (bf16[2,336,256]{2,1,0:T(8,128)(2,1)}, bf16[2,336,256]{2,1,0:T(8,128)(2,1)}, u32[]{:S(2)}, u32[]{:S(2)}) collective-permute-start(bf16[2,336,256]{2,1,0:T(8,128)(2,1)} %get-tuple-element.215), channel_id=1, source_target_pairs={{0,4},{4,0},{8,12},{12,8},{16,20},{20,16},{24,28},{28,24},{1,5},{5... | collective-permute-start | bytes 1032200 | tf_op jit(solution)/shard_map/ppermute | solution.py:34
  103.0 31.7 %collective-permute-start.24 = (bf16[4,336,256]{2,1,0:T(8,128)(2,1)}, bf16[4,336,256]{2,1,0:T(8,128)(2,1)}, u32[]{:S(2)}, u32[]{:S(2)}) collective-permute-start(bf16[4,336,256]{2,1,0:T(8,128)(2,1)} %bitcast.36), channel_id=1, source_target_pairs={{0,8},{4,12},{8,0},{12,4},{16,24},{20,28},{24,16},{28,20},{1,9},{5... | collective-permute-start | bytes 2064392 | tf_op jit(solution)/shard_map/ppermute | solution.py:34
  104.8 27.2 %collective-permute-start.25 = (bf16[2,336,256]{2,1,0:T(8,128)(2,1)}, bf16[2,336,256]{2,1,0:T(8,128)(2,1)}, u32[]{:S(2)}, u32[]{:S(2)}) collective-permute-start(bf16[2,336,256]{2,1,0:T(8,128)(2,1)} %get-tuple-element.213), channel_id=1, source_target_pairs={{0,8},{4,12},{8,0},{12,4},{16,24},{20,28},{24,16},{28,20},{1,9},{5... | collective-permute-start | bytes 1032200 | tf_op jit(solution)/shard_map/ppermute | solution.py:34
  116.8 27.5 %collective-permute-start.22 = (bf16[4,64,1280]{2,1,0:T(8,128)(2,1)S(1)}, bf16[4,64,1280]{2,1,0:T(8,128)(2,1)S(1)}, u32[]{:S(2)}, u32[]{:S(2)}) collective-permute-start(bf16[4,64,1280]{2,1,0:T(8,128)(2,1)S(1)} %get-tuple-element.133), channel_id=1, source_target_pairs={{0,4},{4,0},{8,12},{12,8},{16,20},{20,16},{24,28},{28,24},{1,5},{5... | collective-permute-start | bytes 1966088 | tf_op jit(solution)/shard_map/ppermute | solution.py:34
  120.9 24.4 %collective-permute-start.21 = (bf16[512,512]{1,0:T(8,128)(2,1)S(1)}, bf16[512,512]{1,0:T(8,128)(2,1)S(1)}, u32[]{:S(2)}, u32[]{:S(2)}) collective-permute-start(bf16[512,512]{1,0:T(8,128)(2,1)S(1)} %get-tuple-element.136), channel_id=1, source_target_pairs={{0,2},{2,0},{1,3},{3,1},{4,6},{6,4},{5,7},{7,5},{8,10},{10,8},{9,1... | collective-permute-start | bytes 1572872 | tf_op jit(solution)/shard_map/ppermute | solution.py:29
  122.1 24.7 %collective-permute-start.32 = (bf16[1,336,256]{2,1,0:T(8,128)(2,1)S(1)}, bf16[1,336,256]{2,1,0:T(8,128)(2,1)S(1)}, u32[]{:S(2)}, u32[]{:S(2)}) collective-permute-start(bf16[1,336,256]{2,1,0:T(8,128)(2,1)S(1)} %broadcast_select_fusion.12), channel_id=1, source_target_pairs={{0,16},{4,20},{8,24},{12,28},{16,0},{20,4},{24,8},{28,12},{1,17},{... | collective-permute-start | bytes 516104 | tf_op jit(solution)/shard_map/ppermute | solution.py:34
  145.3 17.5 %collective-permute-start.28 = (bf16[2,64,1280]{2,1,0:T(8,128)(2,1)S(1)}, bf16[2,64,1280]{2,1,0:T(8,128)(2,1)S(1)}, u32[]{:S(2)}, u32[]{:S(2)}) collective-permute-start(bf16[2,64,1280]{2,1,0:T(8,128)(2,1)S(1)} %get-tuple-element.217), channel_id=1, source_target_pairs={{0,8},{4,12},{8,0},{12,4},{16,24},{20,28},{24,16},{28,20},{1,9},{5... | collective-permute-start | bytes 983048 | tf_op jit(solution)/shard_map/ppermute | solution.py:34
  152.3 25.7 %collective-permute-start.38 = (bf16[1,336,256]{2,1,0:T(8,128)(2,1)S(1)}, bf16[1,336,256]{2,1,0:T(8,128)(2,1)S(1)}, u32[]{:S(2)}, u32[]{:S(2)}) collective-permute-start(bf16[1,336,256]{2,1,0:T(8,128)(2,1)S(1)} %add_convert_fusion.13), channel_id=1, source_target_pairs={{0,16},{4,20},{8,24},{12,28},{16,0},{20,4},{24,8},{28,12},{1,17},{... | collective-permute-start | bytes 516104 | tf_op jit(solution)/shard_map/ppermute | solution.py:34
  156.6 25.2 %collective-permute-start.37 = (bf16[1,336,256]{2,1,0:T(8,128)(2,1)S(1)}, bf16[1,336,256]{2,1,0:T(8,128)(2,1)S(1)}, u32[]{:S(2)}, u32[]{:S(2)}) collective-permute-start(bf16[1,336,256]{2,1,0:T(8,128)(2,1)S(1)} %broadcast_select_fusion.10), channel_id=1, source_target_pairs={{0,16},{4,20},{8,24},{12,28},{16,0},{20,4},{24,8},{28,12},{1,17},{... | collective-permute-start | bytes 516104 | tf_op jit(solution)/shard_map/ppermute | solution.py:34
  162.8 20.8 %collective-permute-start.36 = (bf16[1,64,768]{2,1,0:T(8,128)(2,1)S(1)}, bf16[1,64,768]{2,1,0:T(8,128)(2,1)S(1)}, u32[]{:S(2)}, u32[]{:S(2)}) collective-permute-start(bf16[1,64,768]{2,1,0:T(8,128)(2,1)S(1)} %broadcast_select_fusion.14), channel_id=1, source_target_pairs={{0,16},{4,20},{8,24},{12,28},{16,0},{20,4},{24,8},{28,12},{1,17},{... | collective-permute-start | bytes 294920 | tf_op jit(solution)/shard_map/ppermute | solution.py:34
  162.9 22.4 %collective-permute-start.35 = (bf16[1,64,1280]{2,1,0:T(8,128)(2,1)S(1)}, bf16[1,64,1280]{2,1,0:T(8,128)(2,1)S(1)}, u32[]{:S(2)}, u32[]{:S(2)}) collective-permute-start(bf16[1,64,1280]{2,1,0:T(8,128)(2,1)S(1)} %broadcast_select_fusion.13), channel_id=1, source_target_pairs={{0,16},{4,20},{8,24},{12,28},{16,0},{20,4},{24,8},{28,12},{1,17},{... | collective-permute-start | bytes 491528 | tf_op jit(solution)/shard_map/ppermute | solution.py:34
  166.0 21.6 %collective-permute-start.34 = (bf16[512,512]{1,0:T(8,128)(2,1)S(1)}, bf16[512,512]{1,0:T(8,128)(2,1)S(1)}, u32[]{:S(2)}, u32[]{:S(2)}) collective-permute-start(bf16[512,512]{1,0:T(8,128)(2,1)S(1)} %add_convert_fusion.g_own), channel_id=1, source_target_pairs={{0,2},{2,0},{1,3},{3,1},{4,6},{6,4},{5,7},{7,5},{8,10},{10,8},{9,1... | collective-permute-start | bytes 1572872 | tf_op jit(solution)/shard_map/ppermute | solution.py:29
  178.0 42.8 %collective-permute-start.53 = (bf16[2,336,256]{2,1,0:T(8,128)(2,1)S(1)}, bf16[2,336,256]{2,1,0:T(8,128)(2,1)S(1)}, u32[]{:S(2)}, u32[]{:S(2)}) collective-permute-start(bf16[2,336,256]{2,1,0:T(8,128)(2,1)S(1)} %pad_maximum_fusion.4), channel_id=1, source_target_pairs={{0,4},{4,0},{8,12},{12,8},{16,20},{20,16},{24,28},{28,24},{1,5},{5... | collective-permute-start | bytes 1032200 | tf_op jit(solution)/shard_map/ppermute | solution.py:34
  196.1 33.3 %collective-permute-start.33 = (bf16[512,256]{1,0:T(8,128)(2,1)S(1)}, bf16[512,256]{1,0:T(8,128)(2,1)S(1)}, u32[]{:S(2)}, u32[]{:S(2)}) collective-permute-start(bf16[512,256]{1,0:T(8,128)(2,1)S(1)} %get-tuple-element.155), channel_id=1, source_target_pairs={{0,1},{1,0},{2,3},{3,2},{4,5},{5,4},{6,7},{7,6},{8,9},{9,8},{10,11... | collective-permute-start | bytes 786440 | tf_op jit(solution)/shard_map/ppermute | solution.py:29
  205.8 28.5 %collective-permute-start.50 = (bf16[4,336,256]{2,1,0:T(8,128)(2,1)S(1)}, bf16[4,336,256]{2,1,0:T(8,128)(2,1)S(1)}, u32[]{:S(2)}, u32[]{:S(2)}) collective-permute-start(bf16[4,336,256]{2,1,0:T(8,128)(2,1)S(1)} %pad_maximum_fusion.own_first), channel_id=1, source_target_pairs={{0,4},{4,0},{8,12},{12,8},{16,20},{20,16},{24,28},{28,24},{1,5},{5... | collective-permute-start | bytes 2064392 | tf_op jit(solution)/shard_map/ppermute | solution.py:34
  220.9 20.5 %collective-permute-start.55 = (bf16[4,336,256]{2,1,0:T(8,128)(2,1)S(1)}, bf16[4,336,256]{2,1,0:T(8,128)(2,1)S(1)}, u32[]{:S(2)}, u32[]{:S(2)}) collective-permute-start(bf16[4,336,256]{2,1,0:T(8,128)(2,1)S(1)} %pad_maximum_fusion.1.first), channel_id=1, source_target_pairs={{0,8},{4,12},{8,0},{12,4},{16,24},{20,28},{24,16},{28,20},{1,9},{5... | collective-permute-start | bytes 2064392 | tf_op jit(solution)/shard_map/ppermute | solution.py:34
  230.2 24.7 %collective-permute-start.49 = (bf16[4,64,1280]{2,1,0:T(8,128)(2,1)S(1)}, bf16[4,64,1280]{2,1,0:T(8,128)(2,1)S(1)}, u32[]{:S(2)}, u32[]{:S(2)}) collective-permute-start(bf16[4,64,1280]{2,1,0:T(8,128)(2,1)S(1)} %pad_maximum_fusion.2.own_first), channel_id=1, source_target_pairs={{0,4},{4,0},{8,12},{12,8},{16,20},{20,16},{24,28},{28,24},{1,5},{5... | collective-permute-start | bytes 1966088 | tf_op jit(solution)/shard_map/ppermute | solution.py:34
  232.2 19.3 %collective-permute-start.54 = (bf16[4,336,256]{2,1,0:T(8,128)(2,1)S(1)}, bf16[4,336,256]{2,1,0:T(8,128)(2,1)S(1)}, u32[]{:S(2)}, u32[]{:S(2)}) collective-permute-start(bf16[4,336,256]{2,1,0:T(8,128)(2,1)S(1)} %constant_dynamic-update-slice_fusion.4.far_first), channel_id=1, source_target_pairs={{0,8},{4,12},{8,0},{12,4},{16,24},{20,28},{24,16},{28,20},{1,9},{5... | collective-permute-start | bytes 2064392 | tf_op jit(solution)/shard_map/ppermute | solution.py:34
  (76 other events, 658.9 us)
